TPU v7x, 32 devices: a whole 2x2x4 slice. The times are simulated.
32 devices in a mesh: dom: 8 (over y, x, core), head: 4 (over z).
Axes of the slice: x: 2, y: 2, z: 4, core: 2. Of those that a mesh axis runs over, the one named last changes fastest.
Arguments:
- queries: bfloat16 [4608, 2048], P(('dom', 'head')), may hold values from -8 to 8
- keys_in: bfloat16 [4608, 2048], P(('dom', 'head')), may hold values from -8 to 8
- values_in: bfloat16 [4608, 2048], P(('dom', 'head')), may hold values from -6 to 6
- grad_out: bfloat16 [4608, 2048], P(('dom', 'head')), may hold values from -6 to 6
- pos_bias: float32 [32, 64, 576], P('head'), may hold values from -4 to 4
- neighbours: int32 [72, 9], P('dom'), may hold values from 0 to 32, as said below
- send_block: int32 [8, 8, 3], P('dom'), may hold values from 0 to 8, as said below
- orient: int32 [8, 8], P('dom'), may hold values from 0 to 7
Outputs:
- grad_q: bfloat16 [4608, 2048], P(('dom', 'head'))
- grad_k: bfloat16 [4608, 2048], P(('dom', 'head'))
- grad_v: bfloat16 [4608, 2048], P(('dom', 'head'))
Inputs may be any that keep to these rules, and one draw needn't show every extreme that they name: `neighbours`: entry [d * 9 + b, j] names the j-th key block of query block b of domain d: e below 9 is the domain's own block e, and 9 + k * 3 + c is slot c of what domain d borrows from direction k. The 9 entries of a query block are distinct and name only live slots of send_block. `send_block`: entry [p, k, c] is the block that domain p lends in slot c to the domain d with nb(d, k) = p. The live slots of one entry [p, k] name distinct blocks; there are 3 of them for the four edge directions and one for the four corner directions, none where no such d exists; slots that are not live hold 0 and no neighbours entry names them.
All inputs are finite; a program needn't handle non-finite values.
Results may differ from a plain program's by a relative error of at most 0.025.
Values may be sent and summed in bfloat16 or wider, within the bound.
No kernel may reach another device: no remote copies, remote signals or barrier semaphores. Data moves between devices by JAX's collectives and lax.ppermute only.
A program may use at most 128 MiB of HBM per device.

v0:
```python
import functools

import jax
import jax.numpy as jnp
import numpy as np
from jax import lax
from jax.experimental import pallas as pl
from jax.experimental.pallas import tpu as pltpu
from jax.sharding import PartitionSpec as P

HD = 64
PATCH = 8
BT = 64
GRID_ROWS = 4
DIRS = 8
WIN = 9
WINK = 576
QB_DOM = 9
CAP = 3
GROUP_HEADS = 4
SLAB = 32
VMEM_LIMIT = 48 * 1024 * 1024

OFFSET_LIST = [(-1, -1), (-1, 0), (-1, 1), (0, -1), (0, 1), (1, -1), (1, 0), (1, 1)]


class Plan:
    def __init__(self, domains):
        cols = domains // GRID_ROWS
        cells = [divmod(d, cols) for d in range(domains)]
        steps = [(-1, 1)] if cols == 2 else [(-1,), (1,)] if cols > 2 else []
        self.side_pairs = [[(d + step, d) for step in side for d, (_, col) in enumerate(cells)
                            if 0 <= col + step < cols] for side in steps]
        self.rise_pairs = [[(d + step * cols, d) for d, (row, _) in enumerate(cells)
                            if 0 <= row + step < GRID_ROWS] for step in (-1, 1)]
        sides = len(steps)
        self.sides = sides
        self.rise_blocks = CAP + sides
        self.borrowed = sides * CAP + 2 * self.rise_blocks
        self.slots = QB_DOM + self.borrowed
        self.shapes = [CAP] * sides + [self.rise_blocks] * 2
        self.starts = [QB_DOM + sum(self.shapes[:i]) for i in range(len(self.shapes))]
        slot_total = QB_DOM + DIRS * CAP
        self.dir_at = slot_total
        self.lend_at = slot_total + self.borrowed
        table = np.zeros((domains, self.lend_at + 3 * sides), np.int32)
        for d, (_, col) in enumerate(cells):
            table[d, :QB_DOM] = np.arange(QB_DOM)

            def borrow(k, place, count):
                for c in range(CAP):
                    table[d, QB_DOM + k * CAP + c] = place + c % count
                table[d, self.dir_at + place - QB_DOM:self.dir_at + place - QB_DOM + count] = k

            for v, row_step in enumerate((-1, 1)):
                borrow(OFFSET_LIST.index((row_step, 0)), self.starts[sides + v], CAP)
            for i, side in enumerate(steps):
                for step in side:
                    if 0 <= col + step < cols:
                        borrow(OFFSET_LIST.index((0, step)), self.starts[i], CAP)
                        for v, row_step in enumerate((-1, 1)):
                            borrow(OFFSET_LIST.index((row_step, step)), self.starts[sides + v] + CAP + i, 1)
                    if 0 <= col - step < cols:
                        for n, row_step in enumerate((0, -1, 1)):
                            table[d, self.lend_at + 3 * i + n] = OFFSET_LIST.index((row_step, step))
        self.table = table

    def entry(self, table_ref, at):
        return table_ref[lax.axis_index("dom"), at]

    def side_edge(self, i, c, table_ref, send_ref):
        return send_ref[self.entry(table_ref, self.lend_at + 3 * i) * CAP + c]

    def side_corner(self, i, v, table_ref, send_ref):
        k = self.entry(table_ref, self.lend_at + 3 * i + 1 + v)
        found = send_ref[k * CAP]
        for other in range(1, CAP):
            found = jnp.maximum(found, send_ref[k * CAP + other])
        return found

    def rise_edge(self, v, c, send_ref):
        return send_ref[OFFSET_LIST.index((2 * v - 1, 0)) * CAP + c]


def rows_of(c):
    return slice(c * BT, (c + 1) * BT)


def block_rows(index):
    return pl.ds(pl.multiple_of(index * BT, BT), BT)


def turn_matrix(orient, back):
    token = lax.broadcasted_iota(jnp.int32, (BT, BT), 1 if back else 0)
    place = lax.broadcasted_iota(jnp.int32, (BT, BT), 0 if back else 1)
    row, col = token >> 3, token & (PATCH - 1)
    row = jnp.where((orient & 1) == 1, PATCH - 1 - row, row)
    col = jnp.where(((orient >> 1) & 1) == 1, PATCH - 1 - col, col)
    mapped = jnp.where(orient >= 4, PATCH * col + row, PATCH * row + col)
    return (mapped == place).astype(jnp.float32).astype(jnp.bfloat16)


def pack_kernel(parts, left_ref, right_ref, out_ref, *sems):
    holders = out_ref.shape[0]
    width = left_ref.shape[1] // (holders * parts)
    copies = []
    for s in range(holders):
        for part in range(parts):
            at = (s * parts + part) * width
            for ref, to in ((left_ref, 2 * part * width), (right_ref, (2 * part + 1) * width)):
                if sems:
                    copies.append(pltpu.make_async_copy(ref.at[:, at:at + width], out_ref.at[s, :, to:to + width],
                                                        sems[0].at[len(copies)]))
                    copies[-1].start()
                else:
                    out_ref[s, :, to:to + width] = ref[:, at:at + width]
    for copy in copies:
        copy.wait()


def unpack_kernel(parts, dq_ref, dkv_ref, *outs):
    holders = dq_ref.shape[0]
    width = dq_ref.shape[2] // parts
    for s in range(holders):
        for part in range(parts):
            to = slice((s * parts + part) * width, (s * parts + part + 1) * width)
            outs[0][:, to] = dq_ref[s, :, part * width:(part + 1) * width]
            for half in range(2):
                at = (2 * part + half) * width
                outs[1 + half][:, to] = dkv_ref[s, :, at:at + width]


def copy_all(pairs, sems):
    copies = [pltpu.make_async_copy(source, target, sems.at[n]) for n, (source, target) in enumerate(pairs)]
    for copy in copies:
        copy.start()
    for copy in copies:
        copy.wait()


def lend_corners_kernel(plan, table_ref, send_ref, kv_ref, *refs):
    pairs = []
    for i in range(plan.sides):
        for v in range(2):
            block = plan.side_corner(i, v, table_ref, send_ref)
            pairs.append((kv_ref.at[block_rows(block), :], refs[i].at[rows_of(v), :]))
    copy_all(pairs, refs[-1])


def lend_edges_kernel(plan, table_ref, send_ref, kv_ref, *refs):
    corners, out_refs = refs[:plan.sides], refs[plan.sides:]
    pairs = []
    for v in range(2):
        out_ref = out_refs[plan.sides + v]
        for c in range(CAP):
            pairs.append((kv_ref.at[block_rows(plan.rise_edge(v, c, send_ref)), :], out_ref.at[rows_of(c), :]))
        for i in range(plan.sides):
            pairs.append((corners[i].at[rows_of(v), :], out_ref.at[rows_of(CAP + i), :]))
    for i in range(plan.sides):
        for c in range(CAP):
            block = plan.side_edge(i, c, table_ref, send_ref)
            pairs.append((kv_ref.at[block_rows(block), :], out_refs[i].at[rows_of(c), :]))
    copy_all(pairs, refs[-1])


def place_kernel(plan, table_ref, near_ref, orient_ref, places_ref, turns_ref):
    for n in range(QB_DOM * WIN):
        places_ref[n] = plan.entry(table_ref, near_ref[n])
    for n in range(plan.borrowed):
        turns_ref[n] = orient_ref[plan.entry(table_ref, plan.dir_at + n)]


def forward_kernel(plan, *refs):
    for i in range(plan.sides):
        for v in range(2):
            refs[2 + i][rows_of(v), :] = refs[v][rows_of(CAP + i), :]


def settle_kernel(plan, table_ref, send_ref, own_ref, *refs):
    out_ref, total = refs[-2:]
    sides, rises = refs[:plan.sides], refs[plan.sides:plan.sides + 2]
    corners = refs[plan.sides + 2:-2]
    total[...] = own_ref[...]

    def add(block, ref, c):
        total[block_rows(block), :] += ref[rows_of(c), :].astype(jnp.float32)

    for i in range(plan.sides):
        for c in range(CAP):
            add(plan.side_edge(i, c, table_ref, send_ref), sides[i], c)
        for v in range(2):
            add(plan.side_corner(i, v, table_ref, send_ref), corners[i], v)
    for v in range(2):
        for c in range(CAP):
            add(plan.rise_edge(v, c, send_ref), rises[v], c)
    out_ref[...] = total[...].astype(jnp.bfloat16)


def dot(a, b, contract):
    return lax.dot_general(a, b, ((contract[:1], contract[1:]), ((), ())),
                           preferred_element_type=jnp.float32)


def attend_kernel(plan, parts, places_ref, turns_ref, qg_ref, kv_ref, bias_ref, *refs):
    groups = len(plan.shapes)
    arrived = refs[:groups]
    dq_ref, own_ref, *leaving = refs[groups:2 * groups + 2]
    ext, acc, win, wide, scores_ref, dprobs_ref, weights_ref, dscores_ref = refs[2 * groups + 2:]
    width = win.shape[2] // 2
    heads = width // HD
    scale = HD ** -0.5
    keys, values = slice(0, width), slice(width, 2 * width)
    slabs = [slice(at, at + SLAB) for at in range(0, WINK, SLAB)]

    def turned(i, c, back):
        return turn_matrix(turns_ref[plan.starts[i] - QB_DOM + c], back)

    ext[:QB_DOM * BT, :] = kv_ref[...]
    for i, count in enumerate(plan.shapes):
        for c in range(count):
            if c == 0 or c >= CAP:
                turn = turned(i, c, False)
            ext[rows_of(plan.starts[i] + c), :] = dot(turn, arrived[i][rows_of(c), :], (1, 0)).astype(jnp.bfloat16)
    acc[...] = jnp.zeros_like(acc)

    same_head = (lax.broadcasted_iota(jnp.int32, (width, width), 0) // HD
                 == lax.broadcasted_iota(jnp.int32, (width, width), 1) // HD)

    def spread(block):
        copies = jnp.concatenate([block] * heads, axis=0)
        return jnp.where(same_head, copies, jnp.zeros_like(copies))

    def columns(part, half):
        return slice((2 * part + half) * width, (2 * part + half + 1) * width)

    def products(b, part, slot):
        pair = slice(2 * part * width, 2 * (part + 1) * width)
        for j in range(WIN):
            win[slot, rows_of(j), :] = ext[block_rows(places_ref[b * WIN + j]), pair]
        block = qg_ref[block_rows(b), pair]
        wide[slot, 0] = spread(block[:, keys] * jnp.bfloat16(scale))
        wide[slot, 1] = spread(block[:, values])
        bias = bias_ref[:, part * width:(part + 1) * width]
        scores_ref[slot] = dot(win[slot, :, keys], wide[slot, 0], (1, 1)) + bias
        dprobs_ref[slot] = dot(win[slot, :, values], wide[slot, 1], (1, 1)).astype(jnp.bfloat16)

    def softmax(slot):
        top = scores_ref[slot, slabs[0], :]
        for slab in slabs[1:]:
            top = jnp.maximum(top, scores_ref[slot, slab, :])
        top = jnp.max(top, axis=0, keepdims=True)
        total = jnp.zeros((SLAB, width), jnp.float32)
        delta = jnp.zeros((SLAB, width), jnp.float32)
        for slab in slabs:
            weight = jnp.exp(scores_ref[slot, slab, :] - top)
            weights_ref[slot, slab, :] = weight.astype(jnp.bfloat16)
            total = total + weight
            delta = delta + weight * dprobs_ref[slot, slab, :].astype(jnp.float32)
        inverse = 1.0 / jnp.sum(total, axis=0, keepdims=True)
        delta = jnp.sum(delta, axis=0, keepdims=True) * inverse
        for slab in slabs:
            spare = (dprobs_ref[slot, slab, :].astype(jnp.float32) - delta) * inverse
            dscores_ref[slot, slab, :] = (weights_ref[slot, slab, :].astype(jnp.float32) * spare).astype(jnp.bfloat16)
        by_row = jnp.transpose(jnp.broadcast_to(inverse, (8, width)))[:, :1]
        wide[slot, 1] = (wide[slot, 1].astype(jnp.float32) * by_row).astype(jnp.bfloat16)

    def gradients(b, part, slot):
        dscores = dscores_ref[slot]
        grad_q = dot(dscores, win[slot, :, keys], (0, 0))
        grad_q = jnp.where(same_head, grad_q, 0.0)
        total_q = grad_q[:BT]
        for h in range(1, heads):
            total_q = total_q + grad_q[rows_of(h)]
        dq_ref[block_rows(b), part * width:(part + 1) * width] = (total_q * scale).astype(jnp.bfloat16)
        grad_k = dot(dscores, wide[slot, 0], (1, 0))
        grad_v = dot(weights_ref[slot], wide[slot, 1], (1, 0))
        for j in range(WIN):
            place = block_rows(places_ref[b * WIN + j])
            acc[place, columns(part, 0)] += grad_k[rows_of(j)]
            acc[place, columns(part, 1)] += grad_v[rows_of(j)]

    def three_blocks(turn, carry):
        for u in range(3 * parts):
            after, before = u + 1, u - 1
            products(jnp.minimum(3 * turn + after // parts, QB_DOM - 1), after % parts, after % 3)
            softmax(u % 3)
            gradients(jnp.maximum(3 * turn + before // parts, 0), before % parts, before % 3)
        return carry

    for ref in (win, wide, weights_ref, dscores_ref):
        ref[2] = jnp.zeros_like(ref[2])
    products(0, 0, 0)
    lax.fori_loop(0, QB_DOM // 3, three_blocks, 0)
    gradients(QB_DOM - 1, parts - 1, 2)

    own_ref[...] = acc[:QB_DOM * BT, :]
    for i, count in enumerate(plan.shapes):
        for c in range(count):
            if c == 0 or c >= CAP:
                turn = turned(i, c, True)
            slot = acc[rows_of(plan.starts[i] + c), :].astype(jnp.bfloat16)
            leaving[i][rows_of(c), :] = dot(turn, slot, (1, 0)).astype(jnp.bfloat16)


def smem_specs(count):
    return [pl.BlockSpec(memory_space=pltpu.SMEM)] * count


def vmem_specs(count):
    return [pl.BlockSpec(memory_space=pltpu.VMEM)] * count


def params():
    return pltpu.CompilerParams(vmem_limit_bytes=VMEM_LIMIT)


def bf16(*shape):
    return jax.ShapeDtypeStruct(shape, jnp.bfloat16)


def any_specs(count):
    return [pl.BlockSpec(memory_space=pl.ANY)] * count


def busy(microseconds):
    return pl.CostEstimate(flops=int(microseconds * 1.15e9), bytes_accessed=0, transcendentals=0)


def call(kernel, name, scalars, arrays, outs, after=(), in_place=False, out_specs=None, takes=1.0, **more):
    after = [x[tuple(slice(0, n) for n in (1,) * (x.ndim - 2) + (16, 128))] for x in after]
    taken = len(scalars) + len(arrays)

    def body(*refs):
        kernel(*refs[:taken], *refs[taken + len(after):])

    return pl.pallas_call(
        body,
        out_shape=outs,
        in_specs=smem_specs(len(scalars)) + (any_specs if in_place else vmem_specs)(len(arrays)) + any_specs(len(after)),
        out_specs=out_specs or vmem_specs(len(outs)),
        compiler_params=params(),
        cost_estimate=busy(takes),
        name=name,
        **more,
    )(*scalars, *arrays, *after)


def per_device(plan, queries, keys_in, values_in, grad_out, pos_bias, neighbours, send_block, orient):
    heads = pos_bias.shape[0]
    parts = heads // GROUP_HEADS if heads % GROUP_HEADS == 0 else 1
    width = heads * HD
    part_width = width // parts
    tokens = queries.shape[0]
    holders = lax.axis_size("head")
    tokens_dom = tokens * holders
    sides = plan.sides
    table = jnp.asarray(plan.table)
    near, sends, turns = neighbours.reshape(-1), send_block.reshape(-1), orient.reshape(-1)

    def swap(matrix):
        return lax.all_to_all(matrix, "head", split_axis=0, concat_axis=0, tiled=True)

    def swap_back(matrix):
        return swap(matrix.reshape(holders, tokens, -1))

    def pack(left, right, after):
        more = {}
        if part_width % 128 == 0:
            more = dict(in_place=True, scratch_shapes=[pltpu.SemaphoreType.DMA((2 * holders * parts,))])
        return call(functools.partial(pack_kernel, parts), "pack", [], [left, right],
                    [bf16(holders, tokens, 2 * width)], after, **more)[0]

    def permute(value, pairs):
        return lax.ppermute(value, "dom", pairs)

    def permute_back(value, pairs):
        return lax.ppermute(value, "dom", [(d, p) for p, d in pairs])

    block_shapes = [bf16(count * BT, 2 * width) for count in plan.shapes]
    corner_shapes = [bf16(2 * BT, 2 * width)] * sides

    def in_place(copies, outs):
        return dict(in_place=True, out_specs=any_specs(len(outs)), scratch_shapes=[pltpu.SemaphoreType.DMA((copies,))])

    packed_kv = pack(keys_in, values_in, [])
    kv = swap(packed_kv).reshape(tokens_dom, 2 * width)
    bias = jnp.transpose(pos_bias, (2, 0, 1)).reshape(WINK, heads * BT)
    qg = swap(pack(queries, grad_out, [packed_kv, bias])).reshape(tokens_dom, 2 * width)

    corners = call(functools.partial(lend_corners_kernel, plan), "lend_corners", [table, sends], [kv],
                   corner_shapes, **in_place(2 * sides, corner_shapes))
    corners = [permute(x, pairs) for x, pairs in zip(corners, plan.side_pairs)]
    lent = call(functools.partial(lend_edges_kernel, plan), "lend_edges", [table, sends], [kv, *corners], block_shapes,
                **in_place(plan.borrowed, block_shapes))
    arrived = [permute(x, pairs) for x, pairs in zip(lent, plan.side_pairs + plan.rise_pairs)]
    places, turned = call(functools.partial(place_kernel, plan), "place", [table, near, turns], [],
                          [jax.ShapeDtypeStruct((n,), jnp.int32) for n in (QB_DOM * WIN, plan.borrowed)],
                          out_specs=smem_specs(2))

    grad_q, own, *leaving = call(
        functools.partial(attend_kernel, plan, parts), "attend", [places, turned], [qg, kv, bias, *arrived],
        [bf16(tokens_dom, width), jax.ShapeDtypeStruct((tokens_dom, 2 * width), jnp.float32)] + block_shapes,
        takes=15.0,
        scratch_shapes=[
            pltpu.VMEM((plan.slots * BT, 2 * width), jnp.bfloat16),
            pltpu.VMEM((plan.slots * BT, 2 * width), jnp.float32),
            pltpu.VMEM((3, WINK, 2 * part_width), jnp.bfloat16),
            pltpu.VMEM((3, 2, part_width, part_width), jnp.bfloat16),
            pltpu.VMEM((3, WINK, part_width), jnp.float32),
            pltpu.VMEM((3, WINK, part_width), jnp.bfloat16),
            pltpu.VMEM((3, WINK, part_width), jnp.bfloat16),
            pltpu.VMEM((3, WINK, part_width), jnp.bfloat16),
        ],
    )
    rises = [permute_back(x, pairs) for x, pairs in zip(leaving[sides:], plan.rise_pairs)]
    edges = [permute_back(x, pairs) for x, pairs in zip(leaving[:sides], plan.side_pairs)]
    corners = call(functools.partial(forward_kernel, plan), "forward", [], rises, corner_shapes)
    corners = [permute_back(x, pairs) for x, pairs in zip(corners, plan.side_pairs)]
    settled = call(functools.partial(settle_kernel, plan), "settle", [table, sends], [own, *edges, *rises, *corners],
                   [bf16(tokens_dom, 2 * width)],
                   scratch_shapes=[pltpu.VMEM((tokens_dom, 2 * width), jnp.float32)])[0]
    return call(functools.partial(unpack_kernel, parts), "unpack", [], [swap_back(grad_q), swap_back(settled)],
                [bf16(tokens, holders * width)] * 3)


def solution(mesh):
    plan = Plan(mesh.shape["dom"])
    tokens = P(("dom", "head"), None)
    return jax.shard_map(
        functools.partial(per_device, plan),
        mesh=mesh,
        in_specs=(
            tokens,
            tokens,
            tokens,
            tokens,
            P("head", None, None),
            P("dom", None),
            P("dom", None, None),
            P("dom", None),
        ),
        out_specs=(tokens, tokens, tokens),
        check_vma=False,
    )
```

profile of v0, /device:TPU:4, one launch (start us, length us, event | category | flops | bytes accessed | tf_op | source)
XLA Modules:
  0.0 158.6 jit_solution(2741473024910684936)
XLA Ops:
  0.6 0.0 copy-start.2
  0.6 1.1 copy-done.2
  1.7 1.1 copy-done.3
  2.8 1.4 pack.2
  4.2 4.9 %all-to-all-start.1 = ((bf16[4,144,1024]{2,1,0:T(8,128)(2,1)}), bf16[4,144,1024]{2,1,0:T(8,128)(2,1)S(1)}, u32[]{:S(2)}, u32[]{:S(2)}) async-start(bf16[4,144,1024]{2,1,0:T(8,128)(2,1)} %pack.2), calls=%async_computation.1 | async-start | bytes 2359296 | tf_op jit(solution)/shard_map/all_to_all | solution.py:361
  9.0 0.7 slice.8.refs_2_
  9.7 1.8 %copy.14.refs_4_ = f32[576,512]{1,0:T(8,128)S(1)} copy(f32[576,512]{0,1:T(8,128)} %bitcast.14) | data formatting | bytes 2359296 | tf_op jit(solution)/shard_map/reshape | solution.py:387
  11.6 1.5 pack.3
  13.1 0.0 copy-done.9
  13.1 0.0 copy-start.11
  13.1 0.0 copy-start.1
  13.1 24.5 %all-to-all-done.1 = bf16[4,144,1024]{2,1,0:T(8,128)(2,1)S(1)} async-done(((bf16[4,144,1024]{2,1,0:T(8,128)(2,1)}), bf16[4,144,1024]{2,1,0:T(8,128)(2,1)S(1)}, u32[]{:S(2)}, u32[]{:S(2)}) %all-to-all-start.1) | async-done | bytes 1179680 | tf_op jit(solution)/shard_map/all_to_all | solution.py:361
  37.6 3.5 %all-to-all-start = ((bf16[4,144,1024]{2,1,0:T(8,128)(2,1)}), bf16[4,144,1024]{2,1,0:T(8,128)(2,1)S(1)}, u32[]{:S(2)}, u32[]{:S(2)}) async-start(bf16[4,144,1024]{2,1,0:T(8,128)(2,1)} %pack.3), calls=%async_computation | async-start | bytes 2359296 | tf_op jit(solution)/shard_map/all_to_all | solution.py:361
  41.1 0.0 copy-done.11
  41.1 0.1 copy.15
  41.2 0.1 reshape.35.refs_1_
  41.3 1.0 lend_corners.1
  42.3 0.0 copy-start.10
  42.3 0.0 copy-start.8
  42.3 0.1 collective-permute-start
  42.4 1.5 collective-permute-done.refs_3_
  43.9 1.8 %lend_edges.1 = (bf16[192,1024]{1,0:T(8,128)(2,1)}, bf16[256,1024]{1,0:T(8,128)(2,1)}, bf16[256,1024]{1,0:T(8,128)(2,1)}) custom-call(s32[8,47]{1,0:T(8,128)S(1)} %copy-done.1, s32[24]{0:T(128)S(1)} %reshape.35.refs_1_, bf16[576,1024]{1,0:T(8,128)(2,1)S(1)} %bitcast.10, bf16[128,1024]{1,0:T(8,128)(2,1)S(1)} %collective-permute-done.refs_3_), custom_call_target="tpu_custom_call" | custom-call | flops 1150000000 | tf_op jit(solution)/shard_map/lend_edges/pallas_call | solution.py:336
  45.7 3.4 %collective-permute-start.2 = (bf16[256,1024]{1,0:T(8,128)(2,1)}, bf16[256,1024]{1,0:T(8,128)(2,1)S(1)}, u32[]{:S(2)}, u32[]{:S(2)}) collective-permute-start(bf16[256,1024]{1,0:T(8,128)(2,1)} %get-tuple-element.16), channel_id=1, source_target_pairs={{0,8},{4,12},{8,16},{12,20},{16,24},{20,28},{1,9},{5,13},{9,17},{1... | collective-permute-start | bytes 1572872 | tf_op jit(solution)/shard_map/ppermute | solution.py:374
  49.1 3.3 %collective-permute-start.3 = (bf16[256,1024]{1,0:T(8,128)(2,1)}, bf16[256,1024]{1,0:T(8,128)(2,1)}, u32[]{:S(2)}, u32[]{:S(2)}) collective-permute-start(bf16[256,1024]{1,0:T(8,128)(2,1)} %get-tuple-element.17), channel_id=1, source_target_pairs={{8,0},{12,4},{16,8},{20,12},{24,16},{28,20},{9,1},{13,5},{17,9},{2... | collective-permute-start | bytes 1572872 | tf_op jit(solution)/shard_map/ppermute | solution.py:374
  52.5 0.1 collective-permute-start.1
  52.6 0.1 reshape.30.refs_1_
  52.6 1.4 place.1
  54.1 15.1 %all-to-all-done = bf16[4,144,1024]{2,1,0:T(8,128)(2,1)S(1)} async-done(((bf16[4,144,1024]{2,1,0:T(8,128)(2,1)}), bf16[4,144,1024]{2,1,0:T(8,128)(2,1)S(1)}, u32[]{:S(2)}, u32[]{:S(2)}) %all-to-all-start) | async-done | bytes 1179680 | tf_op jit(solution)/shard_map/all_to_all | solution.py:361
  69.1 0.0 collective-permute-done.1.refs_5_
  69.1 0.0 collective-permute-done.2.refs_6_
  69.1 3.0 %collective-permute-done.3.refs_7_ = bf16[256,1024]{1,0:T(8,128)(2,1)} collective-permute-done((bf16[256,1024]{1,0:T(8,128)(2,1)}, bf16[256,1024]{1,0:T(8,128)(2,1)}, u32[]{:S(2)}, u32[]{:S(2)}) %collective-permute-start.3) | collective-permute-done | bytes 524320 | tf_op jit(solution)/shard_map/ppermute | solution.py:374
  72.1 19.4 %attend.1 = (bf16[576,512]{1,0:T(8,128)(2,1)}, f32[576,1024]{1,0:T(8,128)}, bf16[192,1024]{1,0:T(8,128)(2,1)S(1)}, bf16[256,1024]{1,0:T(8,128)(2,1)}, bf16[256,1024]{1,0:T(8,128)(2,1)}) custom-call(s32[81]{0:T(128)S(1)} %get-tuple-element.13.refs_0_, s32[11]{0:T(128)S(1)} %get-tuple-element.14.refs_1_, bf16[576,1024]{1,0:T(8,128)(2,1)S(1)} %bitcast.12, ...), custom_call_target="tpu_custom_call" | custom-call | flops 17250000896 | tf_op jit(solution)/shard_map/attend/pallas_call | solution.py:336
  91.5 0.8 copy-done.6
  92.3 5.4 %collective-permute-start.5 = (bf16[256,1024]{1,0:T(8,128)(2,1)}, bf16[256,1024]{1,0:T(8,128)(2,1)S(1)}, u32[]{:S(2)}, u32[]{:S(2)}) collective-permute-start(bf16[256,1024]{1,0:T(8,128)(2,1)} %get-tuple-element.21), channel_id=1, source_target_pairs={{8,0},{12,4},{16,8},{20,12},{24,16},{28,20},{9,1},{13,5},{17,9},{2... | collective-permute-start | bytes 1572872 | tf_op jit(solution)/shard_map/ppermute | solution.py:377
  97.7 1.9 %collective-permute-start.6 = (bf16[256,1024]{1,0:T(8,128)(2,1)}, bf16[256,1024]{1,0:T(8,128)(2,1)S(1)}, u32[]{:S(2)}, u32[]{:S(2)}) collective-permute-start(bf16[256,1024]{1,0:T(8,128)(2,1)} %get-tuple-element.22), channel_id=1, source_target_pairs={{0,8},{4,12},{8,16},{12,20},{16,24},{20,28},{1,9},{5,13},{9,17},{1... | collective-permute-start | bytes 1572872 | tf_op jit(solution)/shard_map/ppermute | solution.py:377
  99.6 5.1 %all-to-all-start.2 = ((bf16[4,144,512]{2,1,0:T(8,128)(2,1)}), bf16[4,144,512]{2,1,0:T(8,128)(2,1)S(1)}, u32[]{:S(2)}, u32[]{:S(2)}) async-start(bf16[4,144,512]{2,1,0:T(8,128)(2,1)} %bitcast.5), calls=%async_computation.2 | async-start | bytes 1179648 | tf_op jit(solution)/shard_map/all_to_all | solution.py:361
  104.7 0.0 copy-done.7
  104.7 0.0 collective-permute-start.4
  104.7 5.7 %collective-permute-done.5.refs_0_.refs_4_ = bf16[256,1024]{1,0:T(8,128)(2,1)S(1)} collective-permute-done((bf16[256,1024]{1,0:T(8,128)(2,1)}, bf16[256,1024]{1,0:T(8,128)(2,1)S(1)}, u32[]{:S(2)}, u32[]{:S(2)}) %collective-permute-start.5) | collective-permute-done | bytes 524320 | tf_op jit(solution)/shard_map/ppermute | solution.py:377
  110.4 10.4 %collective-permute-done.6.refs_1_.refs_5_ = bf16[256,1024]{1,0:T(8,128)(2,1)S(1)} collective-permute-done((bf16[256,1024]{1,0:T(8,128)(2,1)}, bf16[256,1024]{1,0:T(8,128)(2,1)S(1)}, u32[]{:S(2)}, u32[]{:S(2)}) %collective-permute-start.6) | collective-permute-done | bytes 524320 | tf_op jit(solution)/shard_map/ppermute | solution.py:377
  120.8 0.1 collective-permute-start.7
  120.9 0.0 collective-permute-done.4.refs_3_
  120.9 1.5 collective-permute-done.7.refs_6_
  122.4 0.0 copy-done
  122.4 1.1 settle.1
  123.5 0.0 all-to-all-done.2.refs_0_
  123.6 33.7 %all_to_all.20.refs_1_ = bf16[4,144,1024]{2,1,0:T(8,128)(2,1)S(1)} all-to-all(bf16[4,144,1024]{2,1,0:T(8,128)(2,1)S(1)} %bitcast.8), channel_id=1, replica_groups=mesh['dom'=8,'head'=4] {'head'}, dimensions={0} | all-to-all | bytes 2359296 | tf_op jit(solution)/shard_map/all_to_all | solution.py:361
  157.2 1.4 unpack.1
  (14 shorter events, 0.0 us)
Async XLA Ops:
  0.6 1.1 copy-start.2
  1.7 1.1 copy-start.3
  4.2 33.4 %all-to-all-start.1 = ((bf16[4,144,1024]{2,1,0:T(8,128)(2,1)}), bf16[4,144,1024]{2,1,0:T(8,128)(2,1)S(1)}, u32[]{:S(2)}, u32[]{:S(2)}) async-start(bf16[4,144,1024]{2,1,0:T(8,128)(2,1)} %pack.2), calls=%async_computation.1 | async-start | bytes 2359296 | tf_op jit(solution)/shard_map/all_to_all | solution.py:361
  9.7 1.8 %copy-start.4 = (bf16[144,2048]{1,0:T(8,128)(2,1)S(1)}, bf16[144,2048]{1,0:T(8,128)(2,1)}, u32[]{:S(2)}) copy-start(bf16[144,2048]{1,0:T(8,128)(2,1)} %refs_0_.7) | copy-start | bytes 1769476
  9.7 1.8 %copy-start.5 = (bf16[144,2048]{1,0:T(8,128)(2,1)S(1)}, bf16[144,2048]{1,0:T(8,128)(2,1)}, u32[]{:S(2)}) copy-start(bf16[144,2048]{1,0:T(8,128)(2,1)} %refs_1_.3) | copy-start | bytes 1769476
  11.5 1.5 copy-start.9
  13.1 28.0 %copy-start.11 = (s32[1,8,3]{1,0,2:T(1,128)S(1)}, s32[1,8,3]{1,0,2:T(1,128)}, u32[]{:S(2)}) copy-start(s32[1,8,3]{1,0,2:T(1,128)} %param.15) | copy-start | bytes 292
  13.1 28.2 %copy-start.1 = (s32[8,47]{1,0:T(8,128)S(1)}, s32[8,47]{1,0:T(8,128)}, u32[]{:S(2)}) copy-start(s32[8,47]{1,0:T(8,128)} %constant.2.clone.refs_0_) | copy-start | bytes 4516
  37.6 31.5 %all-to-all-start = ((bf16[4,144,1024]{2,1,0:T(8,128)(2,1)}), bf16[4,144,1024]{2,1,0:T(8,128)(2,1)S(1)}, u32[]{:S(2)}, u32[]{:S(2)}) async-start(bf16[4,144,1024]{2,1,0:T(8,128)(2,1)} %pack.3), calls=%async_computation | async-start | bytes 2359296 | tf_op jit(solution)/shard_map/all_to_all | solution.py:361
  42.3 10.3 %copy-start.10 = (s32[9,9]{1,0:T(8,128)S(1)}, s32[9,9]{1,0:T(8,128)}, u32[]{:S(2)}) copy-start(s32[9,9]{1,0:T(8,128)} %param.14) | copy-start | bytes 976
  42.3 10.3 %copy-start.8 = (s32[1,8]{1,0:T(1,128)S(1)}, s32[1,8]{1,0:T(1,128)}, u32[]{:S(2)}) copy-start(s32[1,8]{1,0:T(1,128)} %param.16) | copy-start | bytes 100
  42.3 1.6 %collective-permute-start = (bf16[128,1024]{1,0:T(8,128)(2,1)S(1)}, bf16[128,1024]{1,0:T(8,128)(2,1)S(1)}, u32[]{:S(2)}, u32[]{:S(2)}) collective-permute-start(bf16[128,1024]{1,0:T(8,128)(2,1)S(1)} %lend_corners.1), channel_id=1, source_target_pairs={{0,4},{8,12},{16,20},{24,28},{4,0},{12,8},{20,16},{28,24},{1,5},{9... | collective-permute-start | bytes 786440 | tf_op jit(solution)/shard_map/ppermute | solution.py:374
  45.7 23.4 %collective-permute-start.2 = (bf16[256,1024]{1,0:T(8,128)(2,1)}, bf16[256,1024]{1,0:T(8,128)(2,1)S(1)}, u32[]{:S(2)}, u32[]{:S(2)}) collective-permute-start(bf16[256,1024]{1,0:T(8,128)(2,1)} %get-tuple-element.16), channel_id=1, source_target_pairs={{0,8},{4,12},{8,16},{12,20},{16,24},{20,28},{1,9},{5,13},{9,17},{1... | collective-permute-start | bytes 1572872 | tf_op jit(solution)/shard_map/ppermute | solution.py:374
  49.1 23.0 %collective-permute-start.3 = (bf16[256,1024]{1,0:T(8,128)(2,1)}, bf16[256,1024]{1,0:T(8,128)(2,1)}, u32[]{:S(2)}, u32[]{:S(2)}) collective-permute-start(bf16[256,1024]{1,0:T(8,128)(2,1)} %get-tuple-element.17), channel_id=1, source_target_pairs={{8,0},{12,4},{16,8},{20,12},{24,16},{28,20},{9,1},{13,5},{17,9},{2... | collective-permute-start | bytes 1572872 | tf_op jit(solution)/shard_map/ppermute | solution.py:374
  52.5 16.7 %collective-permute-start.1 = (bf16[192,1024]{1,0:T(8,128)(2,1)}, bf16[192,1024]{1,0:T(8,128)(2,1)S(1)}, u32[]{:S(2)}, u32[]{:S(2)}) collective-permute-start(bf16[192,1024]{1,0:T(8,128)(2,1)} %get-tuple-element.15), channel_id=1, source_target_pairs={{0,4},{8,12},{16,20},{24,28},{4,0},{12,8},{20,16},{28,24},{1,5},{9... | collective-permute-start | bytes 1179656 | tf_op jit(solution)/shard_map/ppermute | solution.py:374
  91.5 0.8 copy-start.6
  92.3 12.4 %copy-start.7 = (bf16[192,1024]{1,0:T(8,128)(2,1)S(1)}, bf16[192,1024]{1,0:T(8,128)(2,1)}, u32[]{:S(2)}) copy-start(bf16[192,1024]{1,0:T(8,128)(2,1)} %copy-done.6) | copy-start | bytes 1179652
  92.3 18.1 %collective-permute-start.5 = (bf16[256,1024]{1,0:T(8,128)(2,1)}, bf16[256,1024]{1,0:T(8,128)(2,1)S(1)}, u32[]{:S(2)}, u32[]{:S(2)}) collective-permute-start(bf16[256,1024]{1,0:T(8,128)(2,1)} %get-tuple-element.21), channel_id=1, source_target_pairs={{8,0},{12,4},{16,8},{20,12},{24,16},{28,20},{9,1},{13,5},{17,9},{2... | collective-permute-start | bytes 1572872 | tf_op jit(solution)/shard_map/ppermute | solution.py:377
  97.7 23.1 %collective-permute-start.6 = (bf16[256,1024]{1,0:T(8,128)(2,1)}, bf16[256,1024]{1,0:T(8,128)(2,1)S(1)}, u32[]{:S(2)}, u32[]{:S(2)}) collective-permute-start(bf16[256,1024]{1,0:T(8,128)(2,1)} %get-tuple-element.22), channel_id=1, source_target_pairs={{0,8},{4,12},{8,16},{12,20},{16,24},{20,28},{1,9},{5,13},{9,17},{1... | collective-permute-start | bytes 1572872 | tf_op jit(solution)/shard_map/ppermute | solution.py:377
  99.6 23.9 %all-to-all-start.2 = ((bf16[4,144,512]{2,1,0:T(8,128)(2,1)}), bf16[4,144,512]{2,1,0:T(8,128)(2,1)S(1)}, u32[]{:S(2)}, u32[]{:S(2)}) async-start(bf16[4,144,512]{2,1,0:T(8,128)(2,1)} %bitcast.5), calls=%async_computation.2 | async-start | bytes 1179648 | tf_op jit(solution)/shard_map/all_to_all | solution.py:361
  104.7 17.7 %copy-start = (f32[576,1024]{1,0:T(8,128)S(1)}, f32[576,1024]{1,0:T(8,128)}, u32[]{:S(2)}) copy-start(f32[576,1024]{1,0:T(8,128)} %get-tuple-element.19.refs_2_) | copy-start | bytes 7077892
  104.7 16.2 %collective-permute-start.4 = (bf16[192,1024]{1,0:T(8,128)(2,1)S(1)}, bf16[192,1024]{1,0:T(8,128)(2,1)S(1)}, u32[]{:S(2)}, u32[]{:S(2)}) collective-permute-start(bf16[192,1024]{1,0:T(8,128)(2,1)S(1)} %copy-done.7), channel_id=1, source_target_pairs={{4,0},{12,8},{20,16},{28,24},{0,4},{8,12},{16,20},{24,28},{5,1},{1... | collective-permute-start | bytes 1179656 | tf_op jit(solution)/shard_map/ppermute | solution.py:377
  120.8 1.6 %collective-permute-start.7 = (bf16[128,1024]{1,0:T(8,128)(2,1)S(1)}, bf16[128,1024]{1,0:T(8,128)(2,1)S(1)}, u32[]{:S(2)}, u32[]{:S(2)}) collective-permute-start(bf16[128,1024]{1,0:T(8,128)(2,1)S(1)} %forward.1), channel_id=1, source_target_pairs={{4,0},{12,8},{20,16},{28,24},{0,4},{8,12},{16,20},{24,28},{5,1},{1... | collective-permute-start | bytes 786440 | tf_op jit(solution)/shard_map/ppermute | solution.py:377
where the time goes:
time: 159 us
  waiting for transfers between devices  61.7 us (39%)
  blocking collectives  33.7 us (21%)
  Pallas kernels  29 us (18%)
  starting transfers between devices  27.8 us (17%)
  local copies, waits for them, and re-layouts  5.65 us (4%)
    all_to_all x3, waiting for transfers between devices, swap(): lax.all_to_all(matrix, 'head', split_axis=0, concat_axis=0, tiled=True)  39.6 us
    all_to_all x1, blocking collectives, swap(): lax.all_to_all(matrix, 'head', split_axis=0, concat_axis=0, tiled=True)  33.7 us
    pallas_call x9, Pallas kernels, call(): pl.pallas_call(body, out_shape=outs, in_specs=smem_specs(len(scalars)) +...  29 us
    ppermute x4, waiting for transfers between devices, permute_back(): return lax.ppermute(value, 'dom', [(d, p) for p, d in pairs])  17.6 us
    all_to_all x3, starting transfers between devices, swap(): lax.all_to_all(matrix, 'head', split_axis=0, concat_axis=0, tiled=True)  13.5 us
    ppermute x4, starting transfers between devices, permute_back(): return lax.ppermute(value, 'dom', [(d, p) for p, d in pairs])  7.41 us
    ppermute x4, starting transfers between devices, permute(): return lax.ppermute(value, 'dom', pairs)  6.88 us
    ppermute x4, waiting for transfers between devices, permute(): return lax.ppermute(value, 'dom', pairs)  4.53 us
  transfers between devices with their start and end apart: 11, of which 7 were waited for; matrix products, arithmetic and copies ran while one was open for 2% of the time, Pallas kernels for 4%

commit v1 on v0

--- a/solution.py
+++ b/solution.py
@@ -17,7 +17,6 @@
 WINK = 576
 QB_DOM = 9
 CAP = 3
-GROUP_HEADS = 4
 SLAB = 32
 VMEM_LIMIT = 48 * 1024 * 1024
 
@@ -100,34 +99,30 @@
     return (mapped == place).astype(jnp.float32).astype(jnp.bfloat16)
 
 
-def pack_kernel(parts, left_ref, right_ref, out_ref, *sems):
-    holders = out_ref.shape[0]
-    width = left_ref.shape[1] // (holders * parts)
-    copies = []
+def pack_kernel(chunks, chunk, left_ref, right_ref, out_ref, *sems):
+    holders, _, pair_width = out_ref.shape
+    width = pair_width // 2
+    pairs = []
     for s in range(holders):
-        for part in range(parts):
-            at = (s * parts + part) * width
-            for ref, to in ((left_ref, 2 * part * width), (right_ref, (2 * part + 1) * width)):
-                if sems:
-                    copies.append(pltpu.make_async_copy(ref.at[:, at:at + width], out_ref.at[s, :, to:to + width],
-                                                        sems[0].at[len(copies)]))
-                    copies[-1].start()
-                else:
-                    out_ref[s, :, to:to + width] = ref[:, at:at + width]
-    for copy in copies:
-        copy.wait()
-
-
-def unpack_kernel(parts, dq_ref, dkv_ref, *outs):
-    holders = dq_ref.shape[0]
-    width = dq_ref.shape[2] // parts
-    for s in range(holders):
-        for part in range(parts):
-            to = slice((s * parts + part) * width, (s * parts + part + 1) * width)
-            outs[0][:, to] = dq_ref[s, :, part * width:(part + 1) * width]
-            for half in range(2):
-                at = (2 * part + half) * width
-                outs[1 + half][:, to] = dkv_ref[s, :, at:at + width]
+        at = (s * chunks + chunk) * width
+        pairs.append((left_ref.at[:, at:at + width], out_ref.at[s, :, :width]))
+        pairs.append((right_ref.at[:, at:at + width], out_ref.at[s, :, width:]))
+    if sems:
+        copy_all(pairs, sems[0])
+    else:
+        for source, target in pairs:
+            target[...] = source[...]
+
+
+def unpack_kernel(*refs):
+    grads, outs = refs[:-3], refs[-3:]
+    holders, _, all_width = grads[0].shape
+    width = all_width // 3
+    for chunk, grad_ref in enumerate(grads):
+        for s in range(holders):
+            to = slice((s * len(grads) + chunk) * width, (s * len(grads) + chunk + 1) * width)
+            for which, at in enumerate((2 * width, 0, width)):
+                outs[which][:, to] = grad_ref[s, :, at:at + width]
 
 
 def copy_all(pairs, sems):
@@ -179,7 +174,9 @@
 def settle_kernel(plan, table_ref, send_ref, own_ref, *refs):
     out_ref, total = refs[-2:]
     sides, rises = refs[:plan.sides], refs[plan.sides:plan.sides + 2]
-    corners = refs[plan.sides + 2:-2]
+    corners, grad_q_ref = refs[plan.sides + 2:-3], refs[-3]
+    pair_width = own_ref.shape[1]
+    out_ref[:, pair_width:] = grad_q_ref[...]
     total[...] = own_ref[...]
 
     def add(block, ref, c):
@@ -193,7 +190,7 @@
     for v in range(2):
         for c in range(CAP):
             add(plan.rise_edge(v, c, send_ref), rises[v], c)
-    out_ref[...] = total[...].astype(jnp.bfloat16)
+    out_ref[:, :pair_width] = total[...].astype(jnp.bfloat16)
 
 
 def dot(a, b, contract):
@@ -201,7 +198,7 @@
                            preferred_element_type=jnp.float32)
 
 
-def attend_kernel(plan, parts, places_ref, turns_ref, qg_ref, kv_ref, bias_ref, *refs):
+def attend_kernel(plan, places_ref, turns_ref, qg_ref, kv_ref, bias_ref, *refs):
     groups = len(plan.shapes)
     arrived = refs[:groups]
     dq_ref, own_ref, *leaving = refs[groups:2 * groups + 2]
@@ -230,18 +227,15 @@
         copies = jnp.concatenate([block] * heads, axis=0)
         return jnp.where(same_head, copies, jnp.zeros_like(copies))
 
-    def columns(part, half):
-        return slice((2 * part + half) * width, (2 * part + half + 1) * width)
-
-    def products(b, part, slot):
-        pair = slice(2 * part * width, 2 * (part + 1) * width)
+    places = [block_rows(places_ref[n]) for n in range(QB_DOM * WIN)]
+
+    def products(b, slot):
         for j in range(WIN):
-            win[slot, rows_of(j), :] = ext[block_rows(places_ref[b * WIN + j]), pair]
-        block = qg_ref[block_rows(b), pair]
+            win[slot, rows_of(j), :] = ext[places[b * WIN + j], :]
+        block = qg_ref[rows_of(b), :]
         wide[slot, 0] = spread(block[:, keys] * jnp.bfloat16(scale))
         wide[slot, 1] = spread(block[:, values])
-        bias = bias_ref[:, part * width:(part + 1) * width]
-        scores_ref[slot] = dot(win[slot, :, keys], wide[slot, 0], (1, 1)) + bias
+        scores_ref[slot] = dot(win[slot, :, keys], wide[slot, 0], (1, 1)) + bias_ref[...]
         dprobs_ref[slot] = dot(win[slot, :, values], wide[slot, 1], (1, 1)).astype(jnp.bfloat16)
 
     def softmax(slot):
@@ -264,34 +258,28 @@
         by_row = jnp.transpose(jnp.broadcast_to(inverse, (8, width)))[:, :1]
         wide[slot, 1] = (wide[slot, 1].astype(jnp.float32) * by_row).astype(jnp.bfloat16)
 
-    def gradients(b, part, slot):
+    def gradients(b, slot):
         dscores = dscores_ref[slot]
         grad_q = dot(dscores, win[slot, :, keys], (0, 0))
         grad_q = jnp.where(same_head, grad_q, 0.0)
         total_q = grad_q[:BT]
         for h in range(1, heads):
             total_q = total_q + grad_q[rows_of(h)]
-        dq_ref[block_rows(b), part * width:(part + 1) * width] = (total_q * scale).astype(jnp.bfloat16)
+        dq_ref[rows_of(b), :] = (total_q * scale).astype(jnp.bfloat16)
         grad_k = dot(dscores, wide[slot, 0], (1, 0))
         grad_v = dot(weights_ref[slot], wide[slot, 1], (1, 0))
         for j in range(WIN):
-            place = block_rows(places_ref[b * WIN + j])
-            acc[place, columns(part, 0)] += grad_k[rows_of(j)]
-            acc[place, columns(part, 1)] += grad_v[rows_of(j)]
-
-    def three_blocks(turn, carry):
-        for u in range(3 * parts):
-            after, before = u + 1, u - 1
-            products(jnp.minimum(3 * turn + after // parts, QB_DOM - 1), after % parts, after % 3)
-            softmax(u % 3)
-            gradients(jnp.maximum(3 * turn + before // parts, 0), before % parts, before % 3)
-        return carry
-
-    for ref in (win, wide, weights_ref, dscores_ref):
-        ref[2] = jnp.zeros_like(ref[2])
-    products(0, 0, 0)
-    lax.fori_loop(0, QB_DOM // 3, three_blocks, 0)
-    gradients(QB_DOM - 1, parts - 1, 2)
+            acc[places[b * WIN + j], keys] += grad_k[rows_of(j)]
+            acc[places[b * WIN + j], values] += grad_v[rows_of(j)]
+
+    products(0, 0)
+    for b in range(QB_DOM):
+        if b + 1 < QB_DOM:
+            products(b + 1, (b + 1) % 3)
+        softmax(b % 3)
+        if b > 0:
+            gradients(b - 1, (b - 1) % 3)
+    gradients(QB_DOM - 1, (QB_DOM - 1) % 3)
 
     own_ref[...] = acc[:QB_DOM * BT, :]
     for i, count in enumerate(plan.shapes):
@@ -346,28 +334,26 @@
 
 
 def per_device(plan, queries, keys_in, values_in, grad_out, pos_bias, neighbours, send_block, orient):
-    heads = pos_bias.shape[0]
-    parts = heads // GROUP_HEADS if heads % GROUP_HEADS == 0 else 1
+    chunks = 2 if pos_bias.shape[0] % 2 == 0 else 1
+    heads = pos_bias.shape[0] // chunks
     width = heads * HD
-    part_width = width // parts
     tokens = queries.shape[0]
     holders = lax.axis_size("head")
     tokens_dom = tokens * holders
     sides = plan.sides
     table = jnp.asarray(plan.table)
     near, sends, turns = neighbours.reshape(-1), send_block.reshape(-1), orient.reshape(-1)
+    block_shapes = [bf16(count * BT, 2 * width) for count in plan.shapes]
+    corner_shapes = [bf16(2 * BT, 2 * width)] * sides
 
     def swap(matrix):
-        return lax.all_to_all(matrix, "head", split_axis=0, concat_axis=0, tiled=True)
-
-    def swap_back(matrix):
-        return swap(matrix.reshape(holders, tokens, -1))
-
-    def pack(left, right, after):
+        return lax.all_to_all(matrix.reshape(holders, tokens, -1), "head", split_axis=0, concat_axis=0, tiled=True)
+
+    def pack(left, right, chunk, after):
         more = {}
-        if part_width % 128 == 0:
-            more = dict(in_place=True, scratch_shapes=[pltpu.SemaphoreType.DMA((2 * holders * parts,))])
-        return call(functools.partial(pack_kernel, parts), "pack", [], [left, right],
+        if width % 128 == 0:
+            more = dict(in_place=True, scratch_shapes=[pltpu.SemaphoreType.DMA((2 * holders,))])
+        return call(functools.partial(pack_kernel, chunks, chunk), "pack", [], [left, right],
                     [bf16(holders, tokens, 2 * width)], after, **more)[0]
 
     def permute(value, pairs):
@@ -376,51 +362,57 @@
     def permute_back(value, pairs):
         return lax.ppermute(value, "dom", [(d, p) for p, d in pairs])
 
-    block_shapes = [bf16(count * BT, 2 * width) for count in plan.shapes]
-    corner_shapes = [bf16(2 * BT, 2 * width)] * sides
-
     def in_place(copies, outs):
         return dict(in_place=True, out_specs=any_specs(len(outs)), scratch_shapes=[pltpu.SemaphoreType.DMA((copies,))])
 
-    packed_kv = pack(keys_in, values_in, [])
-    kv = swap(packed_kv).reshape(tokens_dom, 2 * width)
-    bias = jnp.transpose(pos_bias, (2, 0, 1)).reshape(WINK, heads * BT)
-    qg = swap(pack(queries, grad_out, [packed_kv, bias])).reshape(tokens_dom, 2 * width)
-
-    corners = call(functools.partial(lend_corners_kernel, plan), "lend_corners", [table, sends], [kv],
-                   corner_shapes, **in_place(2 * sides, corner_shapes))
-    corners = [permute(x, pairs) for x, pairs in zip(corners, plan.side_pairs)]
-    lent = call(functools.partial(lend_edges_kernel, plan), "lend_edges", [table, sends], [kv, *corners], block_shapes,
-                **in_place(plan.borrowed, block_shapes))
-    arrived = [permute(x, pairs) for x, pairs in zip(lent, plan.side_pairs + plan.rise_pairs)]
+    def lend(kv):
+        corners = call(functools.partial(lend_corners_kernel, plan), "lend_corners", [table, sends], [kv],
+                       corner_shapes, **in_place(2 * sides, corner_shapes))
+        corners = [permute(x, pairs) for x, pairs in zip(corners, plan.side_pairs)]
+        lent = call(functools.partial(lend_edges_kernel, plan), "lend_edges", [table, sends], [kv, *corners],
+                    block_shapes, **in_place(plan.borrowed, block_shapes))
+        return lent, [permute(x, pairs) for x, pairs in zip(lent, plan.side_pairs + plan.rise_pairs)]
+
+    def attend(chunk, after):
+        grad_q, own, *leaving = call(
+            functools.partial(attend_kernel, plan), "attend", [places, turned],
+            [qg[chunk], kv[chunk], bias[chunk], *arrived[chunk]],
+            [bf16(tokens_dom, width), jax.ShapeDtypeStruct((tokens_dom, 2 * width), jnp.float32)] + block_shapes,
+            after, takes=8.0,
+            scratch_shapes=[
+                pltpu.VMEM((plan.slots * BT, 2 * width), jnp.bfloat16),
+                pltpu.VMEM((plan.slots * BT, 2 * width), jnp.float32),
+                pltpu.VMEM((3, WINK, 2 * width), jnp.bfloat16),
+                pltpu.VMEM((3, 2, width, width), jnp.bfloat16),
+                pltpu.VMEM((3, WINK, width), jnp.float32),
+                pltpu.VMEM((3, WINK, width), jnp.bfloat16),
+                pltpu.VMEM((3, WINK, width), jnp.bfloat16),
+                pltpu.VMEM((3, WINK, width), jnp.bfloat16),
+            ],
+        )
+        rises = [permute_back(x, pairs) for x, pairs in zip(leaving[sides:], plan.rise_pairs)]
+        edges = [permute_back(x, pairs) for x, pairs in zip(leaving[:sides], plan.side_pairs)]
+        corners = call(functools.partial(forward_kernel, plan), "forward", [], rises, corner_shapes)
+        corners = [permute_back(x, pairs) for x, pairs in zip(corners, plan.side_pairs)]
+        return call(functools.partial(settle_kernel, plan), "settle", [table, sends],
+                    [own, *edges, *rises, *corners, grad_q], [bf16(tokens_dom, 3 * width)],
+                    scratch_shapes=[pltpu.VMEM((tokens_dom, 2 * width), jnp.float32)])[0]
+
     places, turned = call(functools.partial(place_kernel, plan), "place", [table, near, turns], [],
                           [jax.ShapeDtypeStruct((n,), jnp.int32) for n in (QB_DOM * WIN, plan.borrowed)],
                           out_specs=smem_specs(2))
-
-    grad_q, own, *leaving = call(
-        functools.partial(attend_kernel, plan, parts), "attend", [places, turned], [qg, kv, bias, *arrived],
-        [bf16(tokens_dom, width), jax.ShapeDtypeStruct((tokens_dom, 2 * width), jnp.float32)] + block_shapes,
-        takes=15.0,
-        scratch_shapes=[
-            pltpu.VMEM((plan.slots * BT, 2 * width), jnp.bfloat16),
-            pltpu.VMEM((plan.slots * BT, 2 * width), jnp.float32),
-            pltpu.VMEM((3, WINK, 2 * part_width), jnp.bfloat16),
-            pltpu.VMEM((3, 2, part_width, part_width), jnp.bfloat16),
-            pltpu.VMEM((3, WINK, part_width), jnp.float32),
-            pltpu.VMEM((3, WINK, part_width), jnp.bfloat16),
-            pltpu.VMEM((3, WINK, part_width), jnp.bfloat16),
-            pltpu.VMEM((3, WINK, part_width), jnp.bfloat16),
-        ],
-    )
-    rises = [permute_back(x, pairs) for x, pairs in zip(leaving[sides:], plan.rise_pairs)]
-    edges = [permute_back(x, pairs) for x, pairs in zip(leaving[:sides], plan.side_pairs)]
-    corners = call(functools.partial(forward_kernel, plan), "forward", [], rises, corner_shapes)
-    corners = [permute_back(x, pairs) for x, pairs in zip(corners, plan.side_pairs)]
-    settled = call(functools.partial(settle_kernel, plan), "settle", [table, sends], [own, *edges, *rises, *corners],
-                   [bf16(tokens_dom, 2 * width)],
-                   scratch_shapes=[pltpu.VMEM((tokens_dom, 2 * width), jnp.float32)])[0]
-    return call(functools.partial(unpack_kernel, parts), "unpack", [], [swap_back(grad_q), swap_back(settled)],
-                [bf16(tokens, holders * width)] * 3)
+    bias = [jnp.transpose(x, (2, 0, 1)).reshape(WINK, heads * BT) for x in jnp.split(pos_bias, chunks, axis=0)]
+    kv, lent, arrived, qg, packed = [], [], [], [], []
+    for chunk in range(chunks):
+        kv.append(swap(pack(keys_in, values_in, chunk, [])).reshape(tokens_dom, 2 * width))
+        sent, got = lend(kv[chunk])
+        lent.append(sent)
+        arrived.append(got)
+    for chunk in range(chunks):
+        packed.append(pack(queries, grad_out, chunk, [lent[chunk][-1], *(bias if chunk == 0 else [])]))
+        qg.append(swap(packed[chunk]).reshape(tokens_dom, 2 * width))
+    grads = [swap(attend(chunk, packed[chunk + 1:chunk + 2])) for chunk in range(chunks)]
+    return call(unpack_kernel, "unpack", [], grads, [bf16(tokens, holders * chunks * width)] * 3)
 
 
 def solution(mesh):

time: 159 us -> 160 us (level); the launches traced: 159 us -> 158 us
  waiting for transfers between devices: 61.7 us -> 40.8 us
  starting transfers between devices: 27.8 us -> 47.6 us
  blocking collectives: 33.7 us -> 26.8 us
  local copies, waits for them, and re-layouts: 5.65 us -> 10.2 us
  Pallas kernels: 29 us -> 31.2 us
    all_to_all x3 -> x5, waiting for transfers between devices: 39.6 us -> 24.5 us  [swap(): lax.all_to_all(matrix.reshape(holders, tokens, -1), 'head', split_axis=0,...]
    all_to_all x3 -> x5, starting transfers between devices: 13.5 us -> 22 us  [swap(): lax.all_to_all(matrix.reshape(holders, tokens, -1), 'head', split_axis=0,...]
    all_to_all x1, blocking collectives: 33.7 us -> 26.8 us  [swap(): lax.all_to_all(matrix.reshape(holders, tokens, -1), 'head', split_axis=0,...]
    ppermute x4 -> x8, starting transfers between devices: 6.88 us -> 13.6 us  [permute(): return lax.ppermute(value, 'dom', pairs)]
    ppermute x4 -> x8, waiting for transfers between devices: 17.6 us -> 12.8 us  [permute_back(): return lax.ppermute(value, 'dom', [(d, p) for p, d in pairs])]
    ppermute x4 -> x8, starting transfers between devices: 7.41 us -> 12 us  [permute_back(): return lax.ppermute(value, 'dom', [(d, p) for p, d in pairs])]
    pallas_call x9 -> x16, Pallas kernels: 29 us -> 31.2 us  [call(): pl.pallas_call(body, out_shape=outs, in_specs=smem_specs(len(scalars)) +...]
    unnamed x25 -> x29, local copies, waits for them, and re-layouts: 3.01 us -> 4.19 us
  transfers between devices with their start and end apart: 11 -> 21, of which waited for: 7 -> 9; matrix products, arithmetic and copies ran while one was open for 2% -> 4% of each run, Pallas kernels for 4% -> 18%
where the time goes in v1:
time: 160 us; the launch traced here: 158 us
  starting transfers between devices  47.6 us (30%)
  waiting for transfers between devices  40.8 us (25%)
  Pallas kernels  31.2 us (20%)
  blocking collectives  26.8 us (17%)
  local copies, waits for them, and re-layouts  10.2 us (6%)
    pallas_call x16, Pallas kernels, call(): pl.pallas_call(body, out_shape=outs, in_specs=smem_specs(len(scalars)) +...  31.2 us
    all_to_all x1, blocking collectives, swap(): lax.all_to_all(matrix.reshape(holders, tokens, -1), 'head', split_axis=0,...  26.8 us
    all_to_all x5, waiting for transfers between devices, swap(): lax.all_to_all(matrix.reshape(holders, tokens, -1), 'head', split_axis=0,...  24.5 us
    all_to_all x5, starting transfers between devices, swap(): lax.all_to_all(matrix.reshape(holders, tokens, -1), 'head', split_axis=0,...  22 us
    ppermute x8, starting transfers between devices, permute(): return lax.ppermute(value, 'dom', pairs)  13.6 us
    ppermute x8, waiting for transfers between devices, permute_back(): return lax.ppermute(value, 'dom', [(d, p) for p, d in pairs])  12.8 us
    ppermute x8, starting transfers between devices, permute_back(): return lax.ppermute(value, 'dom', [(d, p) for p, d in pairs])  12 us
    unnamed x29, local copies, waits for them, and re-layouts  4.19 us
  transfers between devices with their start and end apart: 21, of which 9 were waited for; matrix products, arithmetic and copies ran while one was open for 4% of the time, Pallas kernels for 18%

profile of v1, /device:TPU:4, one launch (start us, length us, event | category | flops | bytes accessed | tf_op | source)
XLA Modules:
  0.0 157.7 jit_solution(18023567457896057614)
XLA Ops:
  0.6 1.1 copy-done
  1.7 1.1 copy-done.1
  2.8 1.0 pack.6
  3.8 4.9 %all-to-all-start.2 = ((bf16[4,144,512]{2,1,0:T(8,128)(2,1)}), bf16[4,144,512]{2,1,0:T(8,128)(2,1)S(1)}, u32[]{:S(2)}, u32[]{:S(2)}) async-start(bf16[4,144,512]{2,1,0:T(8,128)(2,1)} %pack.6), calls=%async_computation.2 | async-start | bytes 1179648 | tf_op jit(solution)/shard_map/all_to_all | solution.py:350
  8.6 1.0 pack.4
  9.6 14.9 %all-to-all-done.2 = bf16[4,144,512]{2,1,0:T(8,128)(2,1)S(1)} async-done(((bf16[4,144,512]{2,1,0:T(8,128)(2,1)}), bf16[4,144,512]{2,1,0:T(8,128)(2,1)S(1)}, u32[]{:S(2)}, u32[]{:S(2)}) %all-to-all-start.2) | async-done | bytes 589856 | tf_op jit(solution)/shard_map/all_to_all | solution.py:350
  24.5 3.5 %all-to-all-start = ((bf16[4,144,512]{2,1,0:T(8,128)(2,1)}), bf16[4,144,512]{2,1,0:T(8,128)(2,1)S(1)}, u32[]{:S(2)}, u32[]{:S(2)}) async-start(bf16[4,144,512]{2,1,0:T(8,128)(2,1)} %pack.4), calls=%async_computation | async-start | bytes 1179648 | tf_op jit(solution)/shard_map/all_to_all | solution.py:350
  28.2 0.8 lend_corners.3
  29.1 1.3 collective-permute-done.4.refs_3_
  30.5 1.6 %lend_edges.3 = (bf16[192,512]{1,0:T(8,128)(2,1)}, bf16[256,512]{1,0:T(8,128)(2,1)}, bf16[256,512]{1,0:T(8,128)(2,1)}) custom-call(s32[8,47]{1,0:T(8,128)S(1)} %copy-done.10, s32[24]{0:T(128)S(1)} %reshape.39.refs_1_, bf16[576,512]{1,0:T(8,128)(2,1)S(1)} %bitcast.18, bf16[128,512]{1,0:T(8,128)(2,1)S(1)} %collective-permute-done.4.refs_3_), custom_call_target="tpu_custom_call" | custom-call | flops 1150000000 | tf_op jit(solution)/shard_map/lend_edges/pallas_call | solution.py:324
  32.1 0.7 slice.18.refs_2_
  32.7 1.0 pack.7
  33.7 9.7 %all-to-all-done = bf16[4,144,512]{2,1,0:T(8,128)(2,1)S(1)} async-done(((bf16[4,144,512]{2,1,0:T(8,128)(2,1)}), bf16[4,144,512]{2,1,0:T(8,128)(2,1)S(1)}, u32[]{:S(2)}, u32[]{:S(2)}) %all-to-all-start) | async-done | bytes 589856 | tf_op jit(solution)/shard_map/all_to_all | solution.py:350
  43.4 3.5 %all-to-all-start.4 = ((bf16[4,144,512]{2,1,0:T(8,128)(2,1)}), bf16[4,144,512]{2,1,0:T(8,128)(2,1)S(1)}, u32[]{:S(2)}, u32[]{:S(2)}) async-start(bf16[4,144,512]{2,1,0:T(8,128)(2,1)} %pack.7), calls=%async_computation.4 | async-start | bytes 1179648 | tf_op jit(solution)/shard_map/all_to_all | solution.py:350
  46.9 0.8 lend_corners.2
  47.8 0.4 copy-done.11
  48.2 1.2 fusion
  49.5 3.3 %collective-permute-start.11 = (bf16[256,512]{1,0:T(8,128)(2,1)}, bf16[256,512]{1,0:T(8,128)(2,1)}, u32[]{:S(2)}, u32[]{:S(2)}) collective-permute-start(bf16[256,512]{1,0:T(8,128)(2,1)} %get-tuple-element.26), channel_id=1, source_target_pairs={{8,0},{12,4},{16,8},{20,12},{24,16},{28,20},{9,1},{13,5},{17,9},{2... | collective-permute-start | bytes 786440 | tf_op jit(solution)/shard_map/ppermute | solution.py:360
  52.8 3.2 %collective-permute-start.10 = (bf16[256,512]{1,0:T(8,128)(2,1)}, bf16[256,512]{1,0:T(8,128)(2,1)}, u32[]{:S(2)}, u32[]{:S(2)}) collective-permute-start(bf16[256,512]{1,0:T(8,128)(2,1)} %get-tuple-element.33), channel_id=1, source_target_pairs={{0,8},{4,12},{8,16},{12,20},{16,24},{20,28},{1,9},{5,13},{9,17},{1... | collective-permute-start | bytes 786440 | tf_op jit(solution)/shard_map/ppermute | solution.py:360
  56.0 1.4 place.1
  57.4 1.3 copy.17.refs_4_
  58.8 1.3 copy.16.refs_4_
  60.2 0.6 copy-done.7
  60.9 0.9 copy-done.8
  61.8 1.5 lend_edges.2
  63.3 0.7 slice.15.refs_2_
  64.0 1.0 pack.5
  65.0 5.1 %all-to-all-start.1 = ((bf16[4,144,512]{2,1,0:T(8,128)(2,1)}), bf16[4,144,512]{2,1,0:T(8,128)(2,1)S(1)}, u32[]{:S(2)}, u32[]{:S(2)}) async-start(bf16[4,144,512]{2,1,0:T(8,128)(2,1)} %pack.5), calls=%async_computation.1 | async-start | bytes 1179648 | tf_op jit(solution)/shard_map/all_to_all | solution.py:350
  70.1 8.6 %attend.3 = (bf16[576,256]{1,0:T(8,128)(2,1)S(1)}, f32[576,512]{1,0:T(8,128)S(1)}, bf16[192,512]{1,0:T(8,128)(2,1)S(1)}, bf16[256,512]{1,0:T(8,128)(2,1)S(1)}, bf16[256,512]{1,0:T(8,128)(2,1)S(1)}) custom-call(s32[81]{0:T(128)S(1)} %get-tuple-element.21.refs_0_, s32[11]{0:T(128)S(1)} %get-tuple-element.22.refs_1_, bf16[576,512]{1,0:T(8,128)(2,1)S(1)} %bitcast.21, ...), custom_call_target="tpu_custom_call" | custom-call | flops 9200000000 | tf_op jit(solution)/shard_map/attend/pallas_call | solution.py:324
  78.6 3.6 %collective-permute-start.13 = (bf16[256,512]{1,0:T(8,128)(2,1)S(1)}, bf16[256,512]{1,0:T(8,128)(2,1)S(1)}, u32[]{:S(2)}, u32[]{:S(2)}) collective-permute-start(bf16[256,512]{1,0:T(8,128)(2,1)S(1)} %get-tuple-element.36), channel_id=1, source_target_pairs={{8,0},{12,4},{16,8},{20,12},{24,16},{28,20},{9,1},{13,5},{17,9},{2... | collective-permute-start | bytes 786440 | tf_op jit(solution)/shard_map/ppermute | solution.py:363
  82.2 2.3 %collective-permute-start.14 = (bf16[256,512]{1,0:T(8,128)(2,1)S(1)}, bf16[256,512]{1,0:T(8,128)(2,1)S(1)}, u32[]{:S(2)}, u32[]{:S(2)}) collective-permute-start(bf16[256,512]{1,0:T(8,128)(2,1)S(1)} %get-tuple-element.37), channel_id=1, source_target_pairs={{0,8},{4,12},{8,16},{12,20},{16,24},{20,28},{1,9},{5,13},{9,17},{1... | collective-permute-start | bytes 786440 | tf_op jit(solution)/shard_map/ppermute | solution.py:363
  84.5 4.4 %collective-permute-start.3 = (bf16[256,512]{1,0:T(8,128)(2,1)}, bf16[256,512]{1,0:T(8,128)(2,1)S(1)}, u32[]{:S(2)}, u32[]{:S(2)}) collective-permute-start(bf16[256,512]{1,0:T(8,128)(2,1)} %get-tuple-element.23), channel_id=1, source_target_pairs={{8,0},{12,4},{16,8},{20,12},{24,16},{28,20},{9,1},{13,5},{17,9},{2... | collective-permute-start | bytes 786440 | tf_op jit(solution)/shard_map/ppermute | solution.py:360
  89.0 1.9 %collective-permute-start.2 = (bf16[256,512]{1,0:T(8,128)(2,1)}, bf16[256,512]{1,0:T(8,128)(2,1)S(1)}, u32[]{:S(2)}, u32[]{:S(2)}) collective-permute-start(bf16[256,512]{1,0:T(8,128)(2,1)} %get-tuple-element.25), channel_id=1, source_target_pairs={{0,8},{4,12},{8,16},{12,20},{16,24},{20,28},{1,9},{5,13},{9,17},{1... | collective-permute-start | bytes 786440 | tf_op jit(solution)/shard_map/ppermute | solution.py:360
  91.0 4.2 %collective-permute-done.14.refs_1_.refs_5_ = bf16[256,512]{1,0:T(8,128)(2,1)S(1)} collective-permute-done((bf16[256,512]{1,0:T(8,128)(2,1)S(1)}, bf16[256,512]{1,0:T(8,128)(2,1)S(1)}, u32[]{:S(2)}, u32[]{:S(2)}) %collective-permute-start.14) | collective-permute-done | bytes 262176 | tf_op jit(solution)/shard_map/ppermute | solution.py:363
  95.3 0.5 collective-permute-start.1
  95.8 0.7 slice.22.refs_8_
  96.7 1.8 %settle.3 = bf16[576,768]{1,0:T(8,128)(2,1)} custom-call(s32[8,47]{1,0:T(8,128)S(1)} %copy-done.10, s32[24]{0:T(128)S(1)} %reshape.39.refs_1_, f32[576,512]{1,0:T(8,128)S(1)} %get-tuple-element.34.refs_2_, bf16[192,512]{1,0:T(8,128)(2,1)S(1)} %collective-permute-done.12.refs_3_, bf16[256,512]{1,0:T(8,128)(2,1)S(1)} %collective-permute-done.13.refs_0_.refs_4_, ...), custom_call_target="tpu_custom_call" | custom-call | flops 1150000000 | tf_op jit(solution)/shard_map/settle/pallas_call | solution.py:324
  98.5 5.1 %all-to-all-start.5 = ((bf16[4,144,768]{2,1,0:T(8,128)(2,1)}), bf16[4,144,768]{2,1,0:T(8,128)(2,1)S(1)}, u32[]{:S(2)}, u32[]{:S(2)}) async-start(bf16[4,144,768]{2,1,0:T(8,128)(2,1)} %bitcast.10), calls=%async_computation.5 | async-start | bytes 1769472 | tf_op jit(solution)/shard_map/all_to_all | solution.py:350
  103.6 2.1 %collective-permute-done.2.refs_6_ = bf16[256,512]{1,0:T(8,128)(2,1)S(1)} collective-permute-done((bf16[256,512]{1,0:T(8,128)(2,1)}, bf16[256,512]{1,0:T(8,128)(2,1)S(1)}, u32[]{:S(2)}, u32[]{:S(2)}) %collective-permute-start.2) | collective-permute-done | bytes 262176 | tf_op jit(solution)/shard_map/ppermute | solution.py:360
  105.7 8.4 %attend.2 = (bf16[576,256]{1,0:T(8,128)(2,1)S(1)}, f32[576,512]{1,0:T(8,128)S(1)}, bf16[192,512]{1,0:T(8,128)(2,1)S(1)}, bf16[256,512]{1,0:T(8,128)(2,1)S(1)}, bf16[256,512]{1,0:T(8,128)(2,1)S(1)}) custom-call(s32[81]{0:T(128)S(1)} %get-tuple-element.21.refs_0_, s32[11]{0:T(128)S(1)} %get-tuple-element.22.refs_1_, bf16[576,512]{1,0:T(8,128)(2,1)S(1)} %bitcast.20, ...), custom_call_target="tpu_custom_call" | custom-call | flops 9200000000 | tf_op jit(solution)/shard_map/attend/pallas_call | solution.py:324
  114.1 1.9 %collective-permute-start.6 = (bf16[256,512]{1,0:T(8,128)(2,1)S(1)}, bf16[256,512]{1,0:T(8,128)(2,1)S(1)}, u32[]{:S(2)}, u32[]{:S(2)}) collective-permute-start(bf16[256,512]{1,0:T(8,128)(2,1)S(1)} %get-tuple-element.29), channel_id=1, source_target_pairs={{8,0},{12,4},{16,8},{20,12},{24,16},{28,20},{9,1},{13,5},{17,9},{2... | collective-permute-start | bytes 786440 | tf_op jit(solution)/shard_map/ppermute | solution.py:363
  116.0 3.9 %collective-permute-start.7 = (bf16[256,512]{1,0:T(8,128)(2,1)S(1)}, bf16[256,512]{1,0:T(8,128)(2,1)S(1)}, u32[]{:S(2)}, u32[]{:S(2)}) collective-permute-start(bf16[256,512]{1,0:T(8,128)(2,1)S(1)} %get-tuple-element.30), channel_id=1, source_target_pairs={{0,8},{4,12},{8,16},{12,20},{16,24},{20,28},{1,9},{5,13},{9,17},{1... | collective-permute-start | bytes 786440 | tf_op jit(solution)/shard_map/ppermute | solution.py:363
  120.0 3.5 %collective-permute-done.6.refs_0_.refs_4_ = bf16[256,512]{1,0:T(8,128)(2,1)S(1)} collective-permute-done((bf16[256,512]{1,0:T(8,128)(2,1)S(1)}, bf16[256,512]{1,0:T(8,128)(2,1)S(1)}, u32[]{:S(2)}, u32[]{:S(2)}) %collective-permute-start.6) | collective-permute-done | bytes 262176 | tf_op jit(solution)/shard_map/ppermute | solution.py:363
  123.6 3.5 %collective-permute-done.7.refs_1_.refs_5_ = bf16[256,512]{1,0:T(8,128)(2,1)S(1)} collective-permute-done((bf16[256,512]{1,0:T(8,128)(2,1)S(1)}, bf16[256,512]{1,0:T(8,128)(2,1)S(1)}, u32[]{:S(2)}, u32[]{:S(2)}) %collective-permute-start.7) | collective-permute-done | bytes 262176 | tf_op jit(solution)/shard_map/ppermute | solution.py:363
  127.2 1.3 collective-permute-done.8.refs_6_
  128.5 0.9 settle.2
  129.5 26.8 %all_to_all.30.refs_0_ = bf16[4,144,768]{2,1,0:T(8,128)(2,1)S(1)} all-to-all(bf16[4,144,768]{2,1,0:T(8,128)(2,1)S(1)} %bitcast.13), channel_id=1, replica_groups=mesh['dom'=8,'head'=4] {'head'}, dimensions={0} | all-to-all | bytes 1769472 | tf_op jit(solution)/shard_map/all_to_all | solution.py:350
  156.3 1.4 unpack.1
  (50 shorter events, 1.0 us)
Async XLA Ops:
  0.6 1.1 copy-start
  1.7 1.1 copy-start.1
  2.8 5.9 %copy-start.2 = (bf16[144,2048]{1,0:T(8,128)(2,1)S(1)}, bf16[144,2048]{1,0:T(8,128)(2,1)}, u32[]{:S(2)}) copy-start(bf16[144,2048]{1,0:T(8,128)(2,1)} %refs_1_.6) | copy-start | bytes 1769476
  3.8 20.8 %all-to-all-start.2 = ((bf16[4,144,512]{2,1,0:T(8,128)(2,1)}), bf16[4,144,512]{2,1,0:T(8,128)(2,1)S(1)}, u32[]{:S(2)}, u32[]{:S(2)}) async-start(bf16[4,144,512]{2,1,0:T(8,128)(2,1)} %pack.6), calls=%async_computation.2 | async-start | bytes 1179648 | tf_op jit(solution)/shard_map/all_to_all | solution.py:350
  8.6 19.4 %copy-start.13 = (s32[1,8,3]{1,0,2:T(1,128)S(1)}, s32[1,8,3]{1,0,2:T(1,128)}, u32[]{:S(2)}) copy-start(s32[1,8,3]{1,0,2:T(1,128)} %param.15) | copy-start | bytes 292
  8.6 19.6 %copy-start.10 = (s32[8,47]{1,0:T(8,128)S(1)}, s32[8,47]{1,0:T(8,128)}, u32[]{:S(2)}) copy-start(s32[8,47]{1,0:T(8,128)} %constant.2.clone.refs_0_) | copy-start | bytes 4516
  24.5 18.9 %all-to-all-start = ((bf16[4,144,512]{2,1,0:T(8,128)(2,1)}), bf16[4,144,512]{2,1,0:T(8,128)(2,1)S(1)}, u32[]{:S(2)}, u32[]{:S(2)}) async-start(bf16[4,144,512]{2,1,0:T(8,128)(2,1)} %pack.4), calls=%async_computation | async-start | bytes 1179648 | tf_op jit(solution)/shard_map/all_to_all | solution.py:350
  29.0 3.7 %copy-start.3 = (bf16[144,2048]{1,0:T(8,128)(2,1)S(1)}, bf16[144,2048]{1,0:T(8,128)(2,1)}, u32[]{:S(2)}) copy-start(bf16[144,2048]{1,0:T(8,128)(2,1)} %refs_0_.14) | copy-start | bytes 1769476
  29.0 3.7 %copy-start.5 = (bf16[144,2048]{1,0:T(8,128)(2,1)S(1)}, bf16[144,2048]{1,0:T(8,128)(2,1)}, u32[]{:S(2)}) copy-start(bf16[144,2048]{1,0:T(8,128)(2,1)} %refs_1_.7) | copy-start | bytes 1769476
  29.0 1.4 collective-permute-start.4
  43.4 21.6 %all-to-all-start.4 = ((bf16[4,144,512]{2,1,0:T(8,128)(2,1)}), bf16[4,144,512]{2,1,0:T(8,128)(2,1)S(1)}, u32[]{:S(2)}, u32[]{:S(2)}) async-start(bf16[4,144,512]{2,1,0:T(8,128)(2,1)} %pack.7), calls=%async_computation.4 | async-start | bytes 1179648 | tf_op jit(solution)/shard_map/all_to_all | solution.py:350
  46.9 1.3 copy-start.11
  47.7 1.7 %copy-start.12 = (s32[9,9]{1,0:T(8,128)S(1)}, s32[9,9]{1,0:T(8,128)}, u32[]{:S(2)}) copy-start(s32[9,9]{1,0:T(8,128)} %param.14) | copy-start | bytes 976
  47.7 8.3 %copy-start.9 = (s32[1,8]{1,0:T(1,128)S(1)}, s32[1,8]{1,0:T(1,128)}, u32[]{:S(2)}) copy-start(s32[1,8]{1,0:T(1,128)} %param.16) | copy-start | bytes 100
  47.7 12.5 %collective-permute-start = (bf16[128,512]{1,0:T(8,128)(2,1)S(1)}, bf16[128,512]{1,0:T(8,128)(2,1)S(1)}, u32[]{:S(2)}, u32[]{:S(2)}) collective-permute-start(bf16[128,512]{1,0:T(8,128)(2,1)S(1)} %lend_corners.2), channel_id=1, source_target_pairs={{0,4},{8,12},{16,20},{24,28},{4,0},{12,8},{20,16},{28,24},{1,5},{9... | collective-permute-start | bytes 393224 | tf_op jit(solution)/shard_map/ppermute | solution.py:360
  49.5 20.6 %collective-permute-start.11 = (bf16[256,512]{1,0:T(8,128)(2,1)}, bf16[256,512]{1,0:T(8,128)(2,1)}, u32[]{:S(2)}, u32[]{:S(2)}) collective-permute-start(bf16[256,512]{1,0:T(8,128)(2,1)} %get-tuple-element.26), channel_id=1, source_target_pairs={{8,0},{12,4},{16,8},{20,12},{24,16},{28,20},{9,1},{13,5},{17,9},{2... | collective-permute-start | bytes 786440 | tf_op jit(solution)/shard_map/ppermute | solution.py:360
  52.8 17.3 %collective-permute-start.10 = (bf16[256,512]{1,0:T(8,128)(2,1)}, bf16[256,512]{1,0:T(8,128)(2,1)}, u32[]{:S(2)}, u32[]{:S(2)}) collective-permute-start(bf16[256,512]{1,0:T(8,128)(2,1)} %get-tuple-element.33), channel_id=1, source_target_pairs={{0,8},{4,12},{8,16},{12,20},{16,24},{20,28},{1,9},{5,13},{9,17},{1... | collective-permute-start | bytes 786440 | tf_op jit(solution)/shard_map/ppermute | solution.py:360
  60.1 3.9 %copy-start.4 = (bf16[144,2048]{1,0:T(8,128)(2,1)S(1)}, bf16[144,2048]{1,0:T(8,128)(2,1)}, u32[]{:S(2)}) copy-start(bf16[144,2048]{1,0:T(8,128)(2,1)} %refs_0_.14) | copy-start | bytes 1769476
  60.1 3.9 %copy-start.6 = (bf16[144,2048]{1,0:T(8,128)(2,1)S(1)}, bf16[144,2048]{1,0:T(8,128)(2,1)}, u32[]{:S(2)}) copy-start(bf16[144,2048]{1,0:T(8,128)(2,1)} %refs_1_.7) | copy-start | bytes 1769476
  60.1 10.0 %collective-permute-start.9 = (bf16[192,512]{1,0:T(8,128)(2,1)}, bf16[192,512]{1,0:T(8,128)(2,1)}, u32[]{:S(2)}, u32[]{:S(2)}) collective-permute-start(bf16[192,512]{1,0:T(8,128)(2,1)} %get-tuple-element.32), channel_id=1, source_target_pairs={{0,4},{8,12},{16,20},{24,28},{4,0},{12,8},{20,16},{28,24},{1,5},{9... | collective-permute-start | bytes 589832 | tf_op jit(solution)/shard_map/ppermute | solution.py:360
  60.2 0.7 copy-start.7
  60.9 0.9 copy-start.8
  65.0 33.5 %all-to-all-start.1 = ((bf16[4,144,512]{2,1,0:T(8,128)(2,1)}), bf16[4,144,512]{2,1,0:T(8,128)(2,1)S(1)}, u32[]{:S(2)}, u32[]{:S(2)}) async-start(bf16[4,144,512]{2,1,0:T(8,128)(2,1)} %pack.5), calls=%async_computation.1 | async-start | bytes 1179648 | tf_op jit(solution)/shard_map/all_to_all | solution.py:350
  78.6 12.3 %collective-permute-start.13 = (bf16[256,512]{1,0:T(8,128)(2,1)S(1)}, bf16[256,512]{1,0:T(8,128)(2,1)S(1)}, u32[]{:S(2)}, u32[]{:S(2)}) collective-permute-start(bf16[256,512]{1,0:T(8,128)(2,1)S(1)} %get-tuple-element.36), channel_id=1, source_target_pairs={{8,0},{12,4},{16,8},{20,12},{24,16},{28,20},{9,1},{13,5},{17,9},{2... | collective-permute-start | bytes 786440 | tf_op jit(solution)/shard_map/ppermute | solution.py:363
  82.2 13.0 %collective-permute-start.14 = (bf16[256,512]{1,0:T(8,128)(2,1)S(1)}, bf16[256,512]{1,0:T(8,128)(2,1)S(1)}, u32[]{:S(2)}, u32[]{:S(2)}) collective-permute-start(bf16[256,512]{1,0:T(8,128)(2,1)S(1)} %get-tuple-element.37), channel_id=1, source_target_pairs={{0,8},{4,12},{8,16},{12,20},{16,24},{20,28},{1,9},{5,13},{9,17},{1... | collective-permute-start | bytes 786440 | tf_op jit(solution)/shard_map/ppermute | solution.py:363
  84.5 19.1 %collective-permute-start.3 = (bf16[256,512]{1,0:T(8,128)(2,1)}, bf16[256,512]{1,0:T(8,128)(2,1)S(1)}, u32[]{:S(2)}, u32[]{:S(2)}) collective-permute-start(bf16[256,512]{1,0:T(8,128)(2,1)} %get-tuple-element.23), channel_id=1, source_target_pairs={{8,0},{12,4},{16,8},{20,12},{24,16},{28,20},{9,1},{13,5},{17,9},{2... | collective-permute-start | bytes 786440 | tf_op jit(solution)/shard_map/ppermute | solution.py:360
  89.0 16.8 %collective-permute-start.2 = (bf16[256,512]{1,0:T(8,128)(2,1)}, bf16[256,512]{1,0:T(8,128)(2,1)S(1)}, u32[]{:S(2)}, u32[]{:S(2)}) collective-permute-start(bf16[256,512]{1,0:T(8,128)(2,1)} %get-tuple-element.25), channel_id=1, source_target_pairs={{0,8},{4,12},{8,16},{12,20},{16,24},{20,28},{1,9},{5,13},{9,17},{1... | collective-permute-start | bytes 786440 | tf_op jit(solution)/shard_map/ppermute | solution.py:360
  90.9 5.6 %collective-permute-start.12 = (bf16[192,512]{1,0:T(8,128)(2,1)S(1)}, bf16[192,512]{1,0:T(8,128)(2,1)S(1)}, u32[]{:S(2)}, u32[]{:S(2)}) collective-permute-start(bf16[192,512]{1,0:T(8,128)(2,1)S(1)} %get-tuple-element.35), channel_id=1, source_target_pairs={{4,0},{12,8},{20,16},{28,24},{0,4},{8,12},{16,20},{24,28},{5,1},{1... | collective-permute-start | bytes 589832 | tf_op jit(solution)/shard_map/ppermute | solution.py:363
  95.2 1.4 collective-permute-start.15
  95.3 8.3 %collective-permute-start.1 = (bf16[192,512]{1,0:T(8,128)(2,1)}, bf16[192,512]{1,0:T(8,128)(2,1)}, u32[]{:S(2)}, u32[]{:S(2)}) collective-permute-start(bf16[192,512]{1,0:T(8,128)(2,1)} %get-tuple-element.24), channel_id=1, source_target_pairs={{0,4},{8,12},{16,20},{24,28},{4,0},{12,8},{20,16},{28,24},{1,5},{9... | collective-permute-start | bytes 589832 | tf_op jit(solution)/shard_map/ppermute | solution.py:360
  98.5 31.0 %all-to-all-start.5 = ((bf16[4,144,768]{2,1,0:T(8,128)(2,1)}), bf16[4,144,768]{2,1,0:T(8,128)(2,1)S(1)}, u32[]{:S(2)}, u32[]{:S(2)}) async-start(bf16[4,144,768]{2,1,0:T(8,128)(2,1)} %bitcast.10), calls=%async_computation.5 | async-start | bytes 1769472 | tf_op jit(solution)/shard_map/all_to_all | solution.py:350
  114.1 9.5 %collective-permute-start.6 = (bf16[256,512]{1,0:T(8,128)(2,1)S(1)}, bf16[256,512]{1,0:T(8,128)(2,1)S(1)}, u32[]{:S(2)}, u32[]{:S(2)}) collective-permute-start(bf16[256,512]{1,0:T(8,128)(2,1)S(1)} %get-tuple-element.29), channel_id=1, source_target_pairs={{8,0},{12,4},{16,8},{20,12},{24,16},{28,20},{9,1},{13,5},{17,9},{2... | collective-permute-start | bytes 786440 | tf_op jit(solution)/shard_map/ppermute | solution.py:363
  116.0 11.1 %collective-permute-start.7 = (bf16[256,512]{1,0:T(8,128)(2,1)S(1)}, bf16[256,512]{1,0:T(8,128)(2,1)S(1)}, u32[]{:S(2)}, u32[]{:S(2)}) collective-permute-start(bf16[256,512]{1,0:T(8,128)(2,1)S(1)} %get-tuple-element.30), channel_id=1, source_target_pairs={{0,8},{4,12},{8,16},{12,20},{16,24},{20,28},{1,9},{5,13},{9,17},{1... | collective-permute-start | bytes 786440 | tf_op jit(solution)/shard_map/ppermute | solution.py:363
  120.0 7.3 %collective-permute-start.5 = (bf16[192,512]{1,0:T(8,128)(2,1)S(1)}, bf16[192,512]{1,0:T(8,128)(2,1)S(1)}, u32[]{:S(2)}, u32[]{:S(2)}) collective-permute-start(bf16[192,512]{1,0:T(8,128)(2,1)S(1)} %get-tuple-element.28), channel_id=1, source_target_pairs={{4,0},{12,8},{20,16},{28,24},{0,4},{8,12},{16,20},{24,28},{5,1},{1... | collective-permute-start | bytes 589832 | tf_op jit(solution)/shard_map/ppermute | solution.py:363
  127.1 1.4 collective-permute-start.8

commit v2 on v0

--- a/solution.py
+++ b/solution.py
@@ -20,6 +20,7 @@
 GROUP_HEADS = 4
 SLAB = 32
 VMEM_LIMIT = 48 * 1024 * 1024
+VMEM_MOST = 60 * 1024 * 1024
 
 OFFSET_LIST = [(-1, -1), (-1, 0), (-1, 1), (0, -1), (0, 1), (1, -1), (1, 0), (1, 1)]
 
@@ -31,8 +32,9 @@
         steps = [(-1, 1)] if cols == 2 else [(-1,), (1,)] if cols > 2 else []
         self.side_pairs = [[(d + step, d) for step in side for d, (_, col) in enumerate(cells)
                             if 0 <= col + step < cols] for side in steps]
-        self.rise_pairs = [[(d + step * cols, d) for d, (row, _) in enumerate(cells)
-                            if 0 <= row + step < GRID_ROWS] for step in (-1, 1)]
+        rows_apart = [[1 if (row + v) % 2 == 0 else -1 for row, _ in cells] for v in range(2)]
+        self.rise_pairs = [[(d + apart[d] * cols, d) for d, (row, _) in enumerate(cells)
+                            if 0 <= row + apart[d] < GRID_ROWS] for apart in rows_apart]
         sides = len(steps)
         self.sides = sides
         self.rise_blocks = CAP + sides
@@ -43,7 +45,8 @@
         slot_total = QB_DOM + DIRS * CAP
         self.dir_at = slot_total
         self.lend_at = slot_total + self.borrowed
-        table = np.zeros((domains, self.lend_at + 3 * sides), np.int32)
+        self.rise_at = self.lend_at + 3 * sides
+        table = np.zeros((domains, self.rise_at + 2), np.int32)
         for d, (_, col) in enumerate(cells):
             table[d, :QB_DOM] = np.arange(QB_DOM)
 
@@ -52,16 +55,18 @@
                     table[d, QB_DOM + k * CAP + c] = place + c % count
                 table[d, self.dir_at + place - QB_DOM:self.dir_at + place - QB_DOM + count] = k
 
-            for v, row_step in enumerate((-1, 1)):
+            above = [apart[d] for apart in rows_apart]
+            for v, row_step in enumerate(above):
                 borrow(OFFSET_LIST.index((row_step, 0)), self.starts[sides + v], CAP)
+                table[d, self.rise_at + v] = OFFSET_LIST.index((-row_step, 0))
             for i, side in enumerate(steps):
                 for step in side:
                     if 0 <= col + step < cols:
                         borrow(OFFSET_LIST.index((0, step)), self.starts[i], CAP)
-                        for v, row_step in enumerate((-1, 1)):
+                        for v, row_step in enumerate(above):
                             borrow(OFFSET_LIST.index((row_step, step)), self.starts[sides + v] + CAP + i, 1)
                     if 0 <= col - step < cols:
-                        for n, row_step in enumerate((0, -1, 1)):
+                        for n, row_step in enumerate((0, -above[0], -above[1])):
                             table[d, self.lend_at + 3 * i + n] = OFFSET_LIST.index((row_step, step))
         self.table = table
 
@@ -78,8 +83,8 @@
             found = jnp.maximum(found, send_ref[k * CAP + other])
         return found
 
-    def rise_edge(self, v, c, send_ref):
-        return send_ref[OFFSET_LIST.index((2 * v - 1, 0)) * CAP + c]
+    def rise_edge(self, v, c, table_ref, send_ref):
+        return send_ref[self.entry(table_ref, self.rise_at + v) * CAP + c]
 
 
 def rows_of(c):
@@ -153,7 +158,7 @@
     for v in range(2):
         out_ref = out_refs[plan.sides + v]
         for c in range(CAP):
-            pairs.append((kv_ref.at[block_rows(plan.rise_edge(v, c, send_ref)), :], out_ref.at[rows_of(c), :]))
+            pairs.append((kv_ref.at[block_rows(plan.rise_edge(v, c, table_ref, send_ref)), :], out_ref.at[rows_of(c), :]))
         for i in range(plan.sides):
             pairs.append((corners[i].at[rows_of(v), :], out_ref.at[rows_of(CAP + i), :]))
     for i in range(plan.sides):
@@ -192,7 +197,7 @@
             add(plan.side_corner(i, v, table_ref, send_ref), corners[i], v)
     for v in range(2):
         for c in range(CAP):
-            add(plan.rise_edge(v, c, send_ref), rises[v], c)
+            add(plan.rise_edge(v, c, table_ref, send_ref), rises[v], c)
     out_ref[...] = total[...].astype(jnp.bfloat16)
 
 
@@ -205,22 +210,28 @@
     groups = len(plan.shapes)
     arrived = refs[:groups]
     dq_ref, own_ref, *leaving = refs[groups:2 * groups + 2]
-    ext, acc, win, wide, scores_ref, dprobs_ref, weights_ref, dscores_ref = refs[2 * groups + 2:]
-    width = win.shape[2] // 2
+    ext, acc, qg, dq, win, work, probs_ref, dscores_ref = refs[2 * groups + 2:]
+    width = dq.shape[2]
     heads = width // HD
     scale = HD ** -0.5
     keys, values = slice(0, width), slice(width, 2 * width)
+    pairs = [slice(2 * part * width, 2 * (part + 1) * width) for part in range(parts)]
     slabs = [slice(at, at + SLAB) for at in range(0, WINK, SLAB)]
+    places = [block_rows(places_ref[n]) for n in range(QB_DOM * WIN)]
 
     def turned(i, c, back):
         return turn_matrix(turns_ref[plan.starts[i] - QB_DOM + c], back)
 
-    ext[:QB_DOM * BT, :] = kv_ref[...]
+    for part, pair in enumerate(pairs):
+        qg[part] = qg_ref[:, pair]
+        ext[part, :QB_DOM * BT, :] = kv_ref[:, pair]
     for i, count in enumerate(plan.shapes):
         for c in range(count):
             if c == 0 or c >= CAP:
                 turn = turned(i, c, False)
-            ext[rows_of(plan.starts[i] + c), :] = dot(turn, arrived[i][rows_of(c), :], (1, 0)).astype(jnp.bfloat16)
+            block = dot(turn, arrived[i][rows_of(c), :], (1, 0)).astype(jnp.bfloat16)
+            for part, pair in enumerate(pairs):
+                ext[part, rows_of(plan.starts[i] + c), :] = block[:, pair]
     acc[...] = jnp.zeros_like(acc)
 
     same_head = (lax.broadcasted_iota(jnp.int32, (width, width), 0) // HD
@@ -230,76 +241,71 @@
         copies = jnp.concatenate([block] * heads, axis=0)
         return jnp.where(same_head, copies, jnp.zeros_like(copies))
 
-    def columns(part, half):
-        return slice((2 * part + half) * width, (2 * part + half + 1) * width)
-
-    def products(b, part, slot):
-        pair = slice(2 * part * width, 2 * (part + 1) * width)
+    def products(part, b):
+        even = b % 2
         for j in range(WIN):
-            win[slot, rows_of(j), :] = ext[block_rows(places_ref[b * WIN + j]), pair]
-        block = qg_ref[block_rows(b), pair]
-        wide[slot, 0] = spread(block[:, keys] * jnp.bfloat16(scale))
-        wide[slot, 1] = spread(block[:, values])
-        bias = bias_ref[:, part * width:(part + 1) * width]
-        scores_ref[slot] = dot(win[slot, :, keys], wide[slot, 0], (1, 1)) + bias
-        dprobs_ref[slot] = dot(win[slot, :, values], wide[slot, 1], (1, 1)).astype(jnp.bfloat16)
-
-    def softmax(slot):
-        top = scores_ref[slot, slabs[0], :]
+            win[even, rows_of(j), :] = ext[part, places[b * WIN + j], :]
+        query = spread(qg[part, rows_of(b), keys] * jnp.bfloat16(scale))
+        grad = spread(qg[part, rows_of(b), values])
+        work[even, 0] = dot(win[even, :, keys], query, (1, 1)) + bias_ref[part]
+        work[even, 1] = dot(win[even, :, values], grad, (1, 1))
+        return query, grad
+
+    def softmax(b):
+        even = b % 2
+        top = work[even, 0, slabs[0], :]
         for slab in slabs[1:]:
-            top = jnp.maximum(top, scores_ref[slot, slab, :])
+            top = jnp.maximum(top, work[even, 0, slab, :])
         top = jnp.max(top, axis=0, keepdims=True)
         total = jnp.zeros((SLAB, width), jnp.float32)
         delta = jnp.zeros((SLAB, width), jnp.float32)
         for slab in slabs:
-            weight = jnp.exp(scores_ref[slot, slab, :] - top)
-            weights_ref[slot, slab, :] = weight.astype(jnp.bfloat16)
+            weight = jnp.exp(work[even, 0, slab, :] - top)
+            work[even, 0, slab, :] = weight
             total = total + weight
-            delta = delta + weight * dprobs_ref[slot, slab, :].astype(jnp.float32)
+            delta = delta + weight * work[even, 1, slab, :]
         inverse = 1.0 / jnp.sum(total, axis=0, keepdims=True)
         delta = jnp.sum(delta, axis=0, keepdims=True) * inverse
         for slab in slabs:
-            spare = (dprobs_ref[slot, slab, :].astype(jnp.float32) - delta) * inverse
-            dscores_ref[slot, slab, :] = (weights_ref[slot, slab, :].astype(jnp.float32) * spare).astype(jnp.bfloat16)
-        by_row = jnp.transpose(jnp.broadcast_to(inverse, (8, width)))[:, :1]
-        wide[slot, 1] = (wide[slot, 1].astype(jnp.float32) * by_row).astype(jnp.bfloat16)
-
-    def gradients(b, part, slot):
-        dscores = dscores_ref[slot]
-        grad_q = dot(dscores, win[slot, :, keys], (0, 0))
+            probs = work[even, 0, slab, :] * inverse
+            probs_ref[even, slab, :] = probs.astype(jnp.bfloat16)
+            dscores_ref[even, slab, :] = (probs * (work[even, 1, slab, :] - delta)).astype(jnp.bfloat16)
+
+    def gradients(part, b, query, grad):
+        even = b % 2
+        dscores = dscores_ref[even]
+        grad_q = dot(dscores, win[even, :, keys], (0, 0))
         grad_q = jnp.where(same_head, grad_q, 0.0)
         total_q = grad_q[:BT]
         for h in range(1, heads):
             total_q = total_q + grad_q[rows_of(h)]
-        dq_ref[block_rows(b), part * width:(part + 1) * width] = (total_q * scale).astype(jnp.bfloat16)
-        grad_k = dot(dscores, wide[slot, 0], (1, 0))
-        grad_v = dot(weights_ref[slot], wide[slot, 1], (1, 0))
+        dq[part, rows_of(b), :] = (total_q * scale).astype(jnp.bfloat16)
+        grad_k = dot(dscores, query, (1, 0))
+        grad_v = dot(probs_ref[even], grad, (1, 0))
         for j in range(WIN):
-            place = block_rows(places_ref[b * WIN + j])
-            acc[place, columns(part, 0)] += grad_k[rows_of(j)]
-            acc[place, columns(part, 1)] += grad_v[rows_of(j)]
-
-    def three_blocks(turn, carry):
-        for u in range(3 * parts):
-            after, before = u + 1, u - 1
-            products(jnp.minimum(3 * turn + after // parts, QB_DOM - 1), after % parts, after % 3)
-            softmax(u % 3)
-            gradients(jnp.maximum(3 * turn + before // parts, 0), before % parts, before % 3)
+            acc[part, places[b * WIN + j], keys] += grad_k[rows_of(j)]
+            acc[part, places[b * WIN + j], values] += grad_v[rows_of(j)]
+
+    def one_part(part, carry):
+        here = products(part, 0)
+        for b in range(QB_DOM):
+            following = products(part, b + 1) if b + 1 < QB_DOM else None
+            softmax(b)
+            gradients(part, b, *here)
+            here = following
         return carry
 
-    for ref in (win, wide, weights_ref, dscores_ref):
-        ref[2] = jnp.zeros_like(ref[2])
-    products(0, 0, 0)
-    lax.fori_loop(0, QB_DOM // 3, three_blocks, 0)
-    gradients(QB_DOM - 1, parts - 1, 2)
-
-    own_ref[...] = acc[:QB_DOM * BT, :]
+    lax.fori_loop(0, parts, one_part, 0)
+    for part, pair in enumerate(pairs):
+        own_ref[:, pair] = acc[part, :QB_DOM * BT, :]
+        dq_ref[:, part * width:(part + 1) * width] = dq[part]
     for i, count in enumerate(plan.shapes):
         for c in range(count):
             if c == 0 or c >= CAP:
                 turn = turned(i, c, True)
-            slot = acc[rows_of(plan.starts[i] + c), :].astype(jnp.bfloat16)
-            leaving[i][rows_of(c), :] = dot(turn, slot, (1, 0)).astype(jnp.bfloat16)
+            for part, pair in enumerate(pairs):
+                slot = acc[part, rows_of(plan.starts[i] + c), :].astype(jnp.bfloat16)
+                leaving[i][rows_of(c), pair] = dot(turn, slot, (1, 0)).astype(jnp.bfloat16)
 
 
 def smem_specs(count):
@@ -310,8 +316,8 @@
     return [pl.BlockSpec(memory_space=pltpu.VMEM)] * count
 
 
-def params():
-    return pltpu.CompilerParams(vmem_limit_bytes=VMEM_LIMIT)
+def params(limit):
+    return pltpu.CompilerParams(vmem_limit_bytes=limit)
 
 
 def bf16(*shape):
@@ -326,7 +332,7 @@
     return pl.CostEstimate(flops=int(microseconds * 1.15e9), bytes_accessed=0, transcendentals=0)
 
 
-def call(kernel, name, scalars, arrays, outs, after=(), in_place=False, out_specs=None, takes=1.0, **more):
+def call(kernel, name, scalars, arrays, outs, after=(), in_place=False, out_specs=None, takes=1.0, limit=VMEM_LIMIT, **more):
     after = [x[tuple(slice(0, n) for n in (1,) * (x.ndim - 2) + (16, 128))] for x in after]
     taken = len(scalars) + len(arrays)
 
@@ -338,7 +344,7 @@
         out_shape=outs,
         in_specs=smem_specs(len(scalars)) + (any_specs if in_place else vmem_specs)(len(arrays)) + any_specs(len(after)),
         out_specs=out_specs or vmem_specs(len(outs)),
-        compiler_params=params(),
+        compiler_params=params(limit),
         cost_estimate=busy(takes),
         name=name,
         **more,
@@ -366,7 +372,7 @@
     def pack(left, right, after):
         more = {}
         if part_width % 128 == 0:
-            more = dict(in_place=True, scratch_shapes=[pltpu.SemaphoreType.DMA((2 * holders * parts,))])
+            more = dict(in_place=True, limit=VMEM_MOST, scratch_shapes=[pltpu.SemaphoreType.DMA((2 * holders * parts,))])
         return call(functools.partial(pack_kernel, parts), "pack", [], [left, right],
                     [bf16(holders, tokens, 2 * width)], after, **more)[0]
 
@@ -384,7 +390,7 @@
 
     packed_kv = pack(keys_in, values_in, [])
     kv = swap(packed_kv).reshape(tokens_dom, 2 * width)
-    bias = jnp.transpose(pos_bias, (2, 0, 1)).reshape(WINK, heads * BT)
+    bias = jnp.transpose(pos_bias.reshape(parts, heads // parts, BT, WINK), (0, 3, 1, 2)).reshape(parts, WINK, -1)
     qg = swap(pack(queries, grad_out, [packed_kv, bias])).reshape(tokens_dom, 2 * width)
 
     corners = call(functools.partial(lend_corners_kernel, plan), "lend_corners", [table, sends], [kv],
@@ -402,14 +408,14 @@
         [bf16(tokens_dom, width), jax.ShapeDtypeStruct((tokens_dom, 2 * width), jnp.float32)] + block_shapes,
         takes=15.0,
         scratch_shapes=[
-            pltpu.VMEM((plan.slots * BT, 2 * width), jnp.bfloat16),
-            pltpu.VMEM((plan.slots * BT, 2 * width), jnp.float32),
-            pltpu.VMEM((3, WINK, 2 * part_width), jnp.bfloat16),
-            pltpu.VMEM((3, 2, part_width, part_width), jnp.bfloat16),
-            pltpu.VMEM((3, WINK, part_width), jnp.float32),
-            pltpu.VMEM((3, WINK, part_width), jnp.bfloat16),
-            pltpu.VMEM((3, WINK, part_width), jnp.bfloat16),
-            pltpu.VMEM((3, WINK, part_width), jnp.bfloat16),
+            pltpu.VMEM((parts, plan.slots * BT, 2 * part_width), jnp.bfloat16),
+            pltpu.VMEM((parts, plan.slots * BT, 2 * part_width), jnp.float32),
+            pltpu.VMEM((parts, tokens_dom, 2 * part_width), jnp.bfloat16),
+            pltpu.VMEM((parts, tokens_dom, part_width), jnp.bfloat16),
+            pltpu.VMEM((2, WINK, 2 * part_width), jnp.bfloat16),
+            pltpu.VMEM((2, 2, WINK, part_width), jnp.float32),
+            pltpu.VMEM((2, WINK, part_width), jnp.bfloat16),
+            pltpu.VMEM((2, WINK, part_width), jnp.bfloat16),
         ],
     )
     rises = [permute_back(x, pairs) for x, pairs in zip(leaving[sides:], plan.rise_pairs)]

time: 159 us -> 151 us (0.950)
  starting transfers between devices: 27.8 us -> 22.2 us
    ppermute x4, starting transfers between devices: 7.41 us -> 4.56 us  [permute_back(): return lax.ppermute(value, 'dom', [(d, p) for p, d in pairs])]
    ppermute x4, starting transfers between devices: 6.88 us -> 4.07 us  [permute(): return lax.ppermute(value, 'dom', pairs)]
    unnamed x25 -> x17, local copies, waits for them, and re-layouts: 3.01 us -> 0.89 us
    slice x2, local copies, waits for them, and re-layouts: 0.68 us -> 2.56 us  [call(): x[tuple((slice(0, n) for n in (1,) * (x.ndim - 2) + (16, 128)))]]
  transfers between devices with their start and end apart: 11 -> 11, of which waited for: 7 -> 7; matrix products, arithmetic and copies ran while one was open for 2% -> 3% of each run, Pallas kernels for 4% -> 5%
where the time goes in v2:
time: 151 us; the launch traced here: 150 us
  waiting for transfers between devices  60.8 us (40%)
  blocking collectives  33.7 us (22%)
  Pallas kernels  27.8 us (18%)
  starting transfers between devices  22.2 us (15%)
  local copies, waits for them, and re-layouts  5.02 us (3%)
    all_to_all x3, waiting for transfers between devices, swap(): lax.all_to_all(matrix, 'head', split_axis=0, concat_axis=0, tiled=True)  39.9 us
    all_to_all x1, blocking collectives, swap(): lax.all_to_all(matrix, 'head', split_axis=0, concat_axis=0, tiled=True)  33.7 us
    pallas_call x9, Pallas kernels, call(): pl.pallas_call(body, out_shape=outs, in_specs=smem_specs(len(scalars)) +...  27.8 us
    ppermute x4, waiting for transfers between devices, permute_back(): return lax.ppermute(value, 'dom', [(d, p) for p, d in pairs])  17.2 us
    all_to_all x3, starting transfers between devices, swap(): lax.all_to_all(matrix, 'head', split_axis=0, concat_axis=0, tiled=True)  13.6 us
    ppermute x4, starting transfers between devices, permute_back(): return lax.ppermute(value, 'dom', [(d, p) for p, d in pairs])  4.56 us
    ppermute x4, starting transfers between devices, permute(): return lax.ppermute(value, 'dom', pairs)  4.07 us
    ppermute x4, waiting for transfers between devices, permute(): return lax.ppermute(value, 'dom', pairs)  3.65 us
  transfers between devices with their start and end apart: 11, of which 7 were waited for; matrix products, arithmetic and copies ran while one was open for 3% of the time, Pallas kernels for 5%

profile of v2, /device:TPU:4, one launch (start us, length us, event | category | flops | bytes accessed | tf_op | source)
XLA Modules:
  0.0 150.4 jit_solution(13958257295502862897)
XLA Ops:
  0.6 2.5 %pack.2 = bf16[4,144,1024]{2,1,0:T(8,128)(2,1)} custom-call(bf16[144,2048]{1,0:T(8,128)(2,1)} %refs_0_.6, bf16[144,2048]{1,0:T(8,128)(2,1)} %refs_1_.2), custom_call_target="tpu_custom_call" | custom-call | flops 1150000000 | tf_op jit(solution)/shard_map/pack/pallas_call | solution.py:342
  3.2 0.0 copy-start.5
  3.2 5.0 %all-to-all-start.1 = ((bf16[4,144,1024]{2,1,0:T(8,128)(2,1)}), bf16[4,144,1024]{2,1,0:T(8,128)(2,1)S(1)}, u32[]{:S(2)}, u32[]{:S(2)}) async-start(bf16[4,144,1024]{2,1,0:T(8,128)(2,1)} %pack.2), calls=%async_computation.1 | async-start | bytes 2359296 | tf_op jit(solution)/shard_map/all_to_all | solution.py:367
  8.2 1.3 slice.8.refs_2_
  9.4 0.0 copy-done.5
  9.5 1.4 copy.14.refs_4_
  10.9 1.3 slice.9.refs_3_
  12.2 2.5 %pack.3 = bf16[4,144,1024]{2,1,0:T(8,128)(2,1)} custom-call(bf16[144,2048]{1,0:T(8,128)(2,1)} %refs_0_.7, bf16[144,2048]{1,0:T(8,128)(2,1)} %refs_1_.3, bf16[1,16,128]{2,1,0:T(8,128)(2,1)} %slice.8.refs_2_, f32[1,16,128]{2,1,0:T(8,128)} %slice.9.refs_3_), custom_call_target="tpu_custom_call" | custom-call | flops 1150000000 | tf_op jit(solution)/shard_map/pack/pallas_call | solution.py:342
  14.7 0.0 copy-start.7
  14.7 0.0 copy-start.1
  14.7 22.0 %all-to-all-done.1 = bf16[4,144,1024]{2,1,0:T(8,128)(2,1)S(1)} async-done(((bf16[4,144,1024]{2,1,0:T(8,128)(2,1)}), bf16[4,144,1024]{2,1,0:T(8,128)(2,1)S(1)}, u32[]{:S(2)}, u32[]{:S(2)}) %all-to-all-start.1) | async-done | bytes 1179680 | tf_op jit(solution)/shard_map/all_to_all | solution.py:367
  36.7 3.5 %all-to-all-start = ((bf16[4,144,1024]{2,1,0:T(8,128)(2,1)}), bf16[4,144,1024]{2,1,0:T(8,128)(2,1)S(1)}, u32[]{:S(2)}, u32[]{:S(2)}) async-start(bf16[4,144,1024]{2,1,0:T(8,128)(2,1)} %pack.3), calls=%async_computation | async-start | bytes 2359296 | tf_op jit(solution)/shard_map/all_to_all | solution.py:367
  40.3 0.0 copy-done.7
  40.3 0.1 copy.15
  40.3 0.1 reshape.39.refs_1_
  40.4 1.0 lend_corners.1
  41.4 0.0 copy-start.6
  41.4 0.0 copy-start.4
  41.5 0.1 collective-permute-start
  41.5 1.5 %collective-permute-done.refs_3_ = bf16[128,1024]{1,0:T(8,128)(2,1)S(1)} collective-permute-done((bf16[128,1024]{1,0:T(8,128)(2,1)S(1)}, bf16[128,1024]{1,0:T(8,128)(2,1)S(1)}, u32[]{:S(2)}, u32[]{:S(2)}) %collective-permute-start) | collective-permute-done | bytes 262176 | tf_op jit(solution)/shard_map/ppermute | solution.py:380
  43.1 1.8 %lend_edges.1 = (bf16[192,1024]{1,0:T(8,128)(2,1)}, bf16[256,1024]{1,0:T(8,128)(2,1)}, bf16[256,1024]{1,0:T(8,128)(2,1)}) custom-call(s32[8,49]{1,0:T(8,128)S(1)} %copy-done.1, s32[24]{0:T(128)S(1)} %reshape.39.refs_1_, bf16[576,1024]{1,0:T(8,128)(2,1)S(1)} %bitcast.12, bf16[128,1024]{1,0:T(8,128)(2,1)S(1)} %collective-permute-done.refs_3_), custom_call_target="tpu_custom_call" | custom-call | flops 1150000000 | tf_op jit(solution)/shard_map/lend_edges/pallas_call | solution.py:342
  44.9 1.6 %collective-permute-start.2 = (bf16[256,1024]{1,0:T(8,128)(2,1)}, bf16[256,1024]{1,0:T(8,128)(2,1)S(1)}, u32[]{:S(2)}, u32[]{:S(2)}) collective-permute-start(bf16[256,1024]{1,0:T(8,128)(2,1)} %get-tuple-element.16), channel_id=1, source_target_pairs={{8,0},{12,4},{0,8},{4,12},{24,16},{28,20},{16,24},{20,28},{9,1},{1... | collective-permute-start | bytes 1572872 | tf_op jit(solution)/shard_map/ppermute | solution.py:380
  46.4 2.4 %collective-permute-start.3 = (bf16[256,1024]{1,0:T(8,128)(2,1)}, bf16[256,1024]{1,0:T(8,128)(2,1)}, u32[]{:S(2)}, u32[]{:S(2)}) collective-permute-start(bf16[256,1024]{1,0:T(8,128)(2,1)} %get-tuple-element.17), channel_id=1, source_target_pairs={{16,8},{20,12},{8,16},{12,20},{17,9},{21,13},{9,17},{13,21},{18,10... | collective-permute-start | bytes 1572872 | tf_op jit(solution)/shard_map/ppermute | solution.py:380
  48.8 0.1 collective-permute-start.1
  48.9 0.0 copy-done.6
  48.9 0.1 reshape.33.refs_1_
  49.0 0.0 copy-done.4
  49.0 1.4 place.1
  50.4 17.9 %all-to-all-done = bf16[4,144,1024]{2,1,0:T(8,128)(2,1)S(1)} async-done(((bf16[4,144,1024]{2,1,0:T(8,128)(2,1)}), bf16[4,144,1024]{2,1,0:T(8,128)(2,1)S(1)}, u32[]{:S(2)}, u32[]{:S(2)}) %all-to-all-start) | async-done | bytes 1179680 | tf_op jit(solution)/shard_map/all_to_all | solution.py:367
  68.3 0.0 collective-permute-done.1.refs_5_
  68.3 0.0 collective-permute-done.2.refs_6_
  68.3 2.1 %collective-permute-done.3.refs_7_ = bf16[256,1024]{1,0:T(8,128)(2,1)} collective-permute-done((bf16[256,1024]{1,0:T(8,128)(2,1)}, bf16[256,1024]{1,0:T(8,128)(2,1)}, u32[]{:S(2)}, u32[]{:S(2)}) %collective-permute-start.3) | collective-permute-done | bytes 524320 | tf_op jit(solution)/shard_map/ppermute | solution.py:380
  70.4 16.1 %attend.1 = (bf16[576,512]{1,0:T(8,128)(2,1)}, f32[576,1024]{1,0:T(8,128)}, bf16[192,1024]{1,0:T(8,128)(2,1)S(1)}, bf16[256,1024]{1,0:T(8,128)(2,1)}, bf16[256,1024]{1,0:T(8,128)(2,1)}) custom-call(s32[81]{0:T(128)S(1)} %get-tuple-element.13.refs_0_, s32[11]{0:T(128)S(1)} %get-tuple-element.14.refs_1_, bf16[576,1024]{1,0:T(8,128)(2,1)S(1)} %bitcast.14, ...), custom_call_target="tpu_custom_call" | custom-call | flops 17250000896 | tf_op jit(solution)/shard_map/attend/pallas_call | solution.py:342
  86.5 0.8 copy-done.2
  87.3 0.0 collective-permute-start.5
  87.3 4.5 %collective-permute-start.6 = (bf16[256,1024]{1,0:T(8,128)(2,1)}, bf16[256,1024]{1,0:T(8,128)(2,1)S(1)}, u32[]{:S(2)}, u32[]{:S(2)}) collective-permute-start(bf16[256,1024]{1,0:T(8,128)(2,1)} %get-tuple-element.22), channel_id=1, source_target_pairs={{8,16},{12,20},{16,8},{20,12},{9,17},{13,21},{17,9},{21,13},{10,18... | collective-permute-start | bytes 1572872 | tf_op jit(solution)/shard_map/ppermute | solution.py:383
  91.8 5.1 %all-to-all-start.2 = ((bf16[4,144,512]{2,1,0:T(8,128)(2,1)}), bf16[4,144,512]{2,1,0:T(8,128)(2,1)S(1)}, u32[]{:S(2)}, u32[]{:S(2)}) async-start(bf16[4,144,512]{2,1,0:T(8,128)(2,1)} %bitcast.6), calls=%async_computation.2 | async-start | bytes 1179648 | tf_op jit(solution)/shard_map/all_to_all | solution.py:367
  96.8 0.0 copy-done.3
  96.8 0.0 collective-permute-start.4
  96.8 3.8 %collective-permute-done.5.refs_0_.refs_4_ = bf16[256,1024]{1,0:T(8,128)(2,1)S(1)} collective-permute-done((bf16[256,1024]{1,0:T(8,128)(2,1)}, bf16[256,1024]{1,0:T(8,128)(2,1)S(1)}, u32[]{:S(2)}, u32[]{:S(2)}) %collective-permute-start.5) | collective-permute-done | bytes 524320 | tf_op jit(solution)/shard_map/ppermute | solution.py:383
  100.6 11.9 %collective-permute-done.6.refs_1_.refs_5_ = bf16[256,1024]{1,0:T(8,128)(2,1)S(1)} collective-permute-done((bf16[256,1024]{1,0:T(8,128)(2,1)}, bf16[256,1024]{1,0:T(8,128)(2,1)S(1)}, u32[]{:S(2)}, u32[]{:S(2)}) %collective-permute-start.6) | collective-permute-done | bytes 524320 | tf_op jit(solution)/shard_map/ppermute | solution.py:383
  112.6 0.1 collective-permute-start.7
  112.6 0.0 collective-permute-done.4.refs_3_
  112.7 1.5 %collective-permute-done.7.refs_6_ = bf16[128,1024]{1,0:T(8,128)(2,1)S(1)} collective-permute-done((bf16[128,1024]{1,0:T(8,128)(2,1)S(1)}, bf16[128,1024]{1,0:T(8,128)(2,1)S(1)}, u32[]{:S(2)}, u32[]{:S(2)}) %collective-permute-start.7) | collective-permute-done | bytes 262176 | tf_op jit(solution)/shard_map/ppermute | solution.py:383
  114.2 1.1 settle.1
  115.3 0.0 all-to-all-done.2.refs_0_
  115.3 33.7 %all_to_all.20.refs_1_ = bf16[4,144,1024]{2,1,0:T(8,128)(2,1)S(1)} all-to-all(bf16[4,144,1024]{2,1,0:T(8,128)(2,1)S(1)} %bitcast.10), channel_id=1, replica_groups=mesh['dom'=8,'head'=4] {'head'}, dimensions={0} | all-to-all | bytes 2359296 | tf_op jit(solution)/shard_map/all_to_all | solution.py:367
  149.0 1.4 unpack.1
  (6 shorter events, 0.0 us)
Async XLA Ops:
  3.2 6.3 %copy-start.5 = (f32[8,64,576]{2,1,0:T(8,128)S(1)}, f32[8,64,576]{2,1,0:T(8,128)}, u32[]{:S(2)}) copy-start(f32[8,64,576]{2,1,0:T(8,128)} %param.13) | copy-start | bytes 3538948
  3.2 33.5 %all-to-all-start.1 = ((bf16[4,144,1024]{2,1,0:T(8,128)(2,1)}), bf16[4,144,1024]{2,1,0:T(8,128)(2,1)S(1)}, u32[]{:S(2)}, u32[]{:S(2)}) async-start(bf16[4,144,1024]{2,1,0:T(8,128)(2,1)} %pack.2), calls=%async_computation.1 | async-start | bytes 2359296 | tf_op jit(solution)/shard_map/all_to_all | solution.py:367
  14.7 25.6 %copy-start.7 = (s32[1,8,3]{1,0,2:T(1,128)S(1)}, s32[1,8,3]{1,0,2:T(1,128)}, u32[]{:S(2)}) copy-start(s32[1,8,3]{1,0,2:T(1,128)} %param.15) | copy-start | bytes 292
  14.7 25.7 %copy-start.1 = (s32[8,49]{1,0:T(8,128)S(1)}, s32[8,49]{1,0:T(8,128)}, u32[]{:S(2)}) copy-start(s32[8,49]{1,0:T(8,128)} %constant.2.clone.refs_0_) | copy-start | bytes 4708
  36.7 31.5 %all-to-all-start = ((bf16[4,144,1024]{2,1,0:T(8,128)(2,1)}), bf16[4,144,1024]{2,1,0:T(8,128)(2,1)S(1)}, u32[]{:S(2)}, u32[]{:S(2)}) async-start(bf16[4,144,1024]{2,1,0:T(8,128)(2,1)} %pack.3), calls=%async_computation | async-start | bytes 2359296 | tf_op jit(solution)/shard_map/all_to_all | solution.py:367
  41.4 7.5 %copy-start.6 = (s32[9,9]{1,0:T(8,128)S(1)}, s32[9,9]{1,0:T(8,128)}, u32[]{:S(2)}) copy-start(s32[9,9]{1,0:T(8,128)} %param.14) | copy-start | bytes 976
  41.4 7.5 %copy-start.4 = (s32[1,8]{1,0:T(1,128)S(1)}, s32[1,8]{1,0:T(1,128)}, u32[]{:S(2)}) copy-start(s32[1,8]{1,0:T(1,128)} %param.16) | copy-start | bytes 100
  41.5 1.6 %collective-permute-start = (bf16[128,1024]{1,0:T(8,128)(2,1)S(1)}, bf16[128,1024]{1,0:T(8,128)(2,1)S(1)}, u32[]{:S(2)}, u32[]{:S(2)}) collective-permute-start(bf16[128,1024]{1,0:T(8,128)(2,1)S(1)} %lend_corners.1), channel_id=1, source_target_pairs={{0,4},{8,12},{16,20},{24,28},{4,0},{12,8},{20,16},{28,24},{1,5},{9... | collective-permute-start | bytes 786440 | tf_op jit(solution)/shard_map/ppermute | solution.py:380
  44.9 23.4 %collective-permute-start.2 = (bf16[256,1024]{1,0:T(8,128)(2,1)}, bf16[256,1024]{1,0:T(8,128)(2,1)S(1)}, u32[]{:S(2)}, u32[]{:S(2)}) collective-permute-start(bf16[256,1024]{1,0:T(8,128)(2,1)} %get-tuple-element.16), channel_id=1, source_target_pairs={{8,0},{12,4},{0,8},{4,12},{24,16},{28,20},{16,24},{20,28},{9,1},{1... | collective-permute-start | bytes 1572872 | tf_op jit(solution)/shard_map/ppermute | solution.py:380
  46.4 24.0 %collective-permute-start.3 = (bf16[256,1024]{1,0:T(8,128)(2,1)}, bf16[256,1024]{1,0:T(8,128)(2,1)}, u32[]{:S(2)}, u32[]{:S(2)}) collective-permute-start(bf16[256,1024]{1,0:T(8,128)(2,1)} %get-tuple-element.17), channel_id=1, source_target_pairs={{16,8},{20,12},{8,16},{12,20},{17,9},{21,13},{9,17},{13,21},{18,10... | collective-permute-start | bytes 1572872 | tf_op jit(solution)/shard_map/ppermute | solution.py:380
  48.8 19.5 %collective-permute-start.1 = (bf16[192,1024]{1,0:T(8,128)(2,1)}, bf16[192,1024]{1,0:T(8,128)(2,1)S(1)}, u32[]{:S(2)}, u32[]{:S(2)}) collective-permute-start(bf16[192,1024]{1,0:T(8,128)(2,1)} %get-tuple-element.15), channel_id=1, source_target_pairs={{0,4},{8,12},{16,20},{24,28},{4,0},{12,8},{20,16},{28,24},{1,5},{9... | collective-permute-start | bytes 1179656 | tf_op jit(solution)/shard_map/ppermute | solution.py:380
  86.5 0.8 copy-start.2
  87.3 9.6 %copy-start.3 = (bf16[192,1024]{1,0:T(8,128)(2,1)S(1)}, bf16[192,1024]{1,0:T(8,128)(2,1)}, u32[]{:S(2)}) copy-start(bf16[192,1024]{1,0:T(8,128)(2,1)} %copy-done.2) | copy-start | bytes 1179652
  87.3 13.4 %collective-permute-start.5 = (bf16[256,1024]{1,0:T(8,128)(2,1)}, bf16[256,1024]{1,0:T(8,128)(2,1)S(1)}, u32[]{:S(2)}, u32[]{:S(2)}) collective-permute-start(bf16[256,1024]{1,0:T(8,128)(2,1)} %get-tuple-element.21), channel_id=1, source_target_pairs={{0,8},{4,12},{8,0},{12,4},{16,24},{20,28},{24,16},{28,20},{1,9},{5... | collective-permute-start | bytes 1572872 | tf_op jit(solution)/shard_map/ppermute | solution.py:383
  87.3 25.3 %collective-permute-start.6 = (bf16[256,1024]{1,0:T(8,128)(2,1)}, bf16[256,1024]{1,0:T(8,128)(2,1)S(1)}, u32[]{:S(2)}, u32[]{:S(2)}) collective-permute-start(bf16[256,1024]{1,0:T(8,128)(2,1)} %get-tuple-element.22), channel_id=1, source_target_pairs={{8,16},{12,20},{16,8},{20,12},{9,17},{13,21},{17,9},{21,13},{10,18... | collective-permute-start | bytes 1572872 | tf_op jit(solution)/shard_map/ppermute | solution.py:383
  91.8 23.6 %all-to-all-start.2 = ((bf16[4,144,512]{2,1,0:T(8,128)(2,1)}), bf16[4,144,512]{2,1,0:T(8,128)(2,1)S(1)}, u32[]{:S(2)}, u32[]{:S(2)}) async-start(bf16[4,144,512]{2,1,0:T(8,128)(2,1)} %bitcast.6), calls=%async_computation.2 | async-start | bytes 1179648 | tf_op jit(solution)/shard_map/all_to_all | solution.py:367
  96.8 17.4 %copy-start = (f32[576,1024]{1,0:T(8,128)S(1)}, f32[576,1024]{1,0:T(8,128)}, u32[]{:S(2)}) copy-start(f32[576,1024]{1,0:T(8,128)} %get-tuple-element.19.refs_2_) | copy-start | bytes 7077892
  96.8 15.8 %collective-permute-start.4 = (bf16[192,1024]{1,0:T(8,128)(2,1)S(1)}, bf16[192,1024]{1,0:T(8,128)(2,1)S(1)}, u32[]{:S(2)}, u32[]{:S(2)}) collective-permute-start(bf16[192,1024]{1,0:T(8,128)(2,1)S(1)} %copy-done.3), channel_id=1, source_target_pairs={{4,0},{12,8},{20,16},{28,24},{0,4},{8,12},{16,20},{24,28},{5,1},{1... | collective-permute-start | bytes 1179656 | tf_op jit(solution)/shard_map/ppermute | solution.py:383
  112.6 1.6 %collective-permute-start.7 = (bf16[128,1024]{1,0:T(8,128)(2,1)S(1)}, bf16[128,1024]{1,0:T(8,128)(2,1)S(1)}, u32[]{:S(2)}, u32[]{:S(2)}) collective-permute-start(bf16[128,1024]{1,0:T(8,128)(2,1)S(1)} %forward.1), channel_id=1, source_target_pairs={{4,0},{12,8},{20,16},{28,24},{0,4},{8,12},{16,20},{24,28},{5,1},{1... | collective-permute-start | bytes 786440 | tf_op jit(solution)/shard_map/ppermute | solution.py:383

commit v3 on v2

--- a/solution.py
+++ b/solution.py
@@ -123,16 +123,15 @@
         copy.wait()
 
 
-def unpack_kernel(parts, dq_ref, dkv_ref, *outs):
-    holders = dq_ref.shape[0]
-    width = dq_ref.shape[2] // parts
+def unpack_kernel(parts, halves, grad_ref, *outs):
+    holders = grad_ref.shape[0]
+    width = grad_ref.shape[2] // (parts * halves)
     for s in range(holders):
         for part in range(parts):
             to = slice((s * parts + part) * width, (s * parts + part + 1) * width)
-            outs[0][:, to] = dq_ref[s, :, part * width:(part + 1) * width]
-            for half in range(2):
-                at = (2 * part + half) * width
-                outs[1 + half][:, to] = dkv_ref[s, :, at:at + width]
+            for half, out_ref in enumerate(outs):
+                at = (halves * part + half) * width
+                out_ref[:, to] = grad_ref[s, :, at:at + width]
 
 
 def copy_all(pairs, sems):
@@ -181,11 +180,13 @@
             refs[2 + i][rows_of(v), :] = refs[v][rows_of(CAP + i), :]
 
 
-def settle_kernel(plan, table_ref, send_ref, own_ref, *refs):
+def settle_kernel(plan, parts, table_ref, send_ref, *refs):
     out_ref, total = refs[-2:]
-    sides, rises = refs[:plan.sides], refs[plan.sides:plan.sides + 2]
-    corners = refs[plan.sides + 2:-2]
-    total[...] = own_ref[...]
+    sides, rises = refs[parts:parts + plan.sides], refs[parts + plan.sides:parts + plan.sides + 2]
+    corners = refs[parts + plan.sides + 2:-2]
+    for part in range(parts):
+        columns = refs[part].shape[1]
+        total[:, part * columns:(part + 1) * columns] = refs[part][...]
 
     def add(block, ref, c):
         total[block_rows(block), :] += ref[rows_of(c), :].astype(jnp.float32)
@@ -206,47 +207,48 @@
                            preferred_element_type=jnp.float32)
 
 
-def attend_kernel(plan, parts, places_ref, turns_ref, qg_ref, kv_ref, bias_ref, *refs):
+def attend_kernel(plan, part, places_ref, turns_ref, qg_ref, kv_ref, bias_ref, *refs):
     groups = len(plan.shapes)
-    arrived = refs[:groups]
-    dq_ref, own_ref, *leaving = refs[groups:2 * groups + 2]
-    ext, acc, qg, dq, win, work, probs_ref, dscores_ref = refs[2 * groups + 2:]
-    width = dq.shape[2]
+    arrived, refs = refs[:groups], refs[groups:]
+    given, refs = (refs[:groups + 1], refs[groups + 1:]) if part > 0 else ([], refs)
+    own_ref, dq_ref, *leaving = refs[:groups + 2]
+    ext, acc, mask, win, work, probs_ref, dscores_ref = refs[groups + 2:]
+    width = probs_ref.shape[2]
     heads = width // HD
     scale = HD ** -0.5
     keys, values = slice(0, width), slice(width, 2 * width)
-    pairs = [slice(2 * part * width, 2 * (part + 1) * width) for part in range(parts)]
+    mine = slice(2 * part * width, 2 * (part + 1) * width)
+    query_lanes = slice(2 * part * width, (2 * part + 1) * width)
+    grad_lanes = slice((2 * part + 1) * width, 2 * (part + 1) * width)
     slabs = [slice(at, at + SLAB) for at in range(0, WINK, SLAB)]
     places = [block_rows(places_ref[n]) for n in range(QB_DOM * WIN)]
 
     def turned(i, c, back):
         return turn_matrix(turns_ref[plan.starts[i] - QB_DOM + c], back)
 
-    for part, pair in enumerate(pairs):
-        qg[part] = qg_ref[:, pair]
-        ext[part, :QB_DOM * BT, :] = kv_ref[:, pair]
+    for source, target in zip(given, [dq_ref, *leaving]):
+        target[:, :source.shape[1]] = source[...]
+    ext[:QB_DOM * BT, :] = kv_ref[:, mine]
     for i, count in enumerate(plan.shapes):
         for c in range(count):
             if c == 0 or c >= CAP:
                 turn = turned(i, c, False)
-            block = dot(turn, arrived[i][rows_of(c), :], (1, 0)).astype(jnp.bfloat16)
-            for part, pair in enumerate(pairs):
-                ext[part, rows_of(plan.starts[i] + c), :] = block[:, pair]
+            ext[rows_of(plan.starts[i] + c), :] = dot(turn, arrived[i][rows_of(c), mine], (1, 0)).astype(jnp.bfloat16)
     acc[...] = jnp.zeros_like(acc)
 
     same_head = (lax.broadcasted_iota(jnp.int32, (width, width), 0) // HD
                  == lax.broadcasted_iota(jnp.int32, (width, width), 1) // HD)
+    mask[...] = same_head.astype(jnp.float32).astype(jnp.bfloat16)
 
     def spread(block):
-        copies = jnp.concatenate([block] * heads, axis=0)
-        return jnp.where(same_head, copies, jnp.zeros_like(copies))
-
-    def products(part, b):
+        return jnp.concatenate([block] * heads, axis=0) * mask[...]
+
+    def products(b):
         even = b % 2
         for j in range(WIN):
-            win[even, rows_of(j), :] = ext[part, places[b * WIN + j], :]
-        query = spread(qg[part, rows_of(b), keys] * jnp.bfloat16(scale))
-        grad = spread(qg[part, rows_of(b), values])
+            win[even, rows_of(j), :] = ext[places[b * WIN + j], :]
+        query = spread(qg_ref[rows_of(b), query_lanes] * jnp.bfloat16(scale))
+        grad = spread(qg_ref[rows_of(b), grad_lanes])
         work[even, 0] = dot(win[even, :, keys], query, (1, 1)) + bias_ref[part]
         work[even, 1] = dot(win[even, :, values], grad, (1, 1))
         return query, grad
@@ -271,7 +273,7 @@
             probs_ref[even, slab, :] = probs.astype(jnp.bfloat16)
             dscores_ref[even, slab, :] = (probs * (work[even, 1, slab, :] - delta)).astype(jnp.bfloat16)
 
-    def gradients(part, b, query, grad):
+    def gradients(b, query, grad):
         even = b % 2
         dscores = dscores_ref[even]
         grad_q = dot(dscores, win[even, :, keys], (0, 0))
@@ -279,33 +281,27 @@
         total_q = grad_q[:BT]
         for h in range(1, heads):
             total_q = total_q + grad_q[rows_of(h)]
-        dq[part, rows_of(b), :] = (total_q * scale).astype(jnp.bfloat16)
+        dq_ref[rows_of(b), part * width:(part + 1) * width] = (total_q * scale).astype(jnp.bfloat16)
         grad_k = dot(dscores, query, (1, 0))
         grad_v = dot(probs_ref[even], grad, (1, 0))
         for j in range(WIN):
-            acc[part, places[b * WIN + j], keys] += grad_k[rows_of(j)]
-            acc[part, places[b * WIN + j], values] += grad_v[rows_of(j)]
-
-    def one_part(part, carry):
-        here = products(part, 0)
-        for b in range(QB_DOM):
-            following = products(part, b + 1) if b + 1 < QB_DOM else None
-            softmax(b)
-            gradients(part, b, *here)
-            here = following
-        return carry
-
-    lax.fori_loop(0, parts, one_part, 0)
-    for part, pair in enumerate(pairs):
-        own_ref[:, pair] = acc[part, :QB_DOM * BT, :]
-        dq_ref[:, part * width:(part + 1) * width] = dq[part]
+            acc[places[b * WIN + j], keys] += grad_k[rows_of(j)]
+            acc[places[b * WIN + j], values] += grad_v[rows_of(j)]
+
+    here = products(0)
+    for b in range(QB_DOM):
+        following = products(b + 1) if b + 1 < QB_DOM else None
+        softmax(b)
+        gradients(b, *here)
+        here = following
+
+    own_ref[...] = acc[:QB_DOM * BT, :]
     for i, count in enumerate(plan.shapes):
         for c in range(count):
             if c == 0 or c >= CAP:
                 turn = turned(i, c, True)
-            for part, pair in enumerate(pairs):
-                slot = acc[part, rows_of(plan.starts[i] + c), :].astype(jnp.bfloat16)
-                leaving[i][rows_of(c), pair] = dot(turn, slot, (1, 0)).astype(jnp.bfloat16)
+            slot = acc[rows_of(plan.starts[i] + c), :].astype(jnp.bfloat16)
+            leaving[i][rows_of(c), mine] = dot(turn, slot, (1, 0)).astype(jnp.bfloat16)
 
 
 def smem_specs(count):
@@ -403,30 +399,39 @@
                           [jax.ShapeDtypeStruct((n,), jnp.int32) for n in (QB_DOM * WIN, plan.borrowed)],
                           out_specs=smem_specs(2))
 
-    grad_q, own, *leaving = call(
-        functools.partial(attend_kernel, plan, parts), "attend", [places, turned], [qg, kv, bias, *arrived],
-        [bf16(tokens_dom, width), jax.ShapeDtypeStruct((tokens_dom, 2 * width), jnp.float32)] + block_shapes,
-        takes=15.0,
-        scratch_shapes=[
-            pltpu.VMEM((parts, plan.slots * BT, 2 * part_width), jnp.bfloat16),
-            pltpu.VMEM((parts, plan.slots * BT, 2 * part_width), jnp.float32),
-            pltpu.VMEM((parts, tokens_dom, 2 * part_width), jnp.bfloat16),
-            pltpu.VMEM((parts, tokens_dom, part_width), jnp.bfloat16),
-            pltpu.VMEM((2, WINK, 2 * part_width), jnp.bfloat16),
-            pltpu.VMEM((2, 2, WINK, part_width), jnp.float32),
-            pltpu.VMEM((2, WINK, part_width), jnp.bfloat16),
-            pltpu.VMEM((2, WINK, part_width), jnp.bfloat16),
-        ],
-    )
+    owns, given = [], []
+    for part in range(parts):
+        done = (part + 1) * part_width
+        own, *given = call(
+            functools.partial(attend_kernel, plan, part), "attend", [places, turned],
+            [qg, kv, bias, *arrived, *given],
+            [jax.ShapeDtypeStruct((tokens_dom, 2 * part_width), jnp.float32), bf16(tokens_dom, done)]
+            + [bf16(count * BT, 2 * done) for count in plan.shapes],
+            takes=8.0,
+            scratch_shapes=[
+                pltpu.VMEM((plan.slots * BT, 2 * part_width), jnp.bfloat16),
+                pltpu.VMEM((plan.slots * BT, 2 * part_width), jnp.float32),
+                pltpu.VMEM((part_width, part_width), jnp.bfloat16),
+                pltpu.VMEM((2, WINK, 2 * part_width), jnp.bfloat16),
+                pltpu.VMEM((2, 2, WINK, part_width), jnp.float32),
+                pltpu.VMEM((2, WINK, part_width), jnp.bfloat16),
+                pltpu.VMEM((2, WINK, part_width), jnp.bfloat16),
+            ],
+        )
+        owns.append(own)
+    grad_q, *leaving = given
     rises = [permute_back(x, pairs) for x, pairs in zip(leaving[sides:], plan.rise_pairs)]
     edges = [permute_back(x, pairs) for x, pairs in zip(leaving[:sides], plan.side_pairs)]
     corners = call(functools.partial(forward_kernel, plan), "forward", [], rises, corner_shapes)
     corners = [permute_back(x, pairs) for x, pairs in zip(corners, plan.side_pairs)]
-    settled = call(functools.partial(settle_kernel, plan), "settle", [table, sends], [own, *edges, *rises, *corners],
+    settled = call(functools.partial(settle_kernel, plan, parts), "settle", [table, sends], [*owns, *edges, *rises, *corners],
                    [bf16(tokens_dom, 2 * width)],
                    scratch_shapes=[pltpu.VMEM((tokens_dom, 2 * width), jnp.float32)])[0]
-    return call(functools.partial(unpack_kernel, parts), "unpack", [], [swap_back(grad_q), swap_back(settled)],
-                [bf16(tokens, holders * width)] * 3)
+    grads = []
+    for halves, grad in ((1, grad_q), (2, settled)):
+        grads += call(functools.partial(unpack_kernel, parts, halves), "unpack", [], [swap_back(grad)],
+                      [bf16(tokens, holders * width)] * halves)
+    return tuple(grads)
 
 
 def solution(mesh):

time: 151 us -> 158 us (1.046)
  blocking collectives: 33.7 us -> 0 us
  waiting for transfers between devices: 60.8 us -> 88 us
  starting transfers between devices: 22.2 us -> 27.1 us
  Pallas kernels: 27.8 us -> 32.3 us
  local copies, waits for them, and re-layouts: 5.02 us -> 8.73 us
    all_to_all x1 -> x0, blocking collectives: 33.7 us -> none  [swap(): lax.all_to_all(matrix, 'head', split_axis=0, concat_axis=0, tiled=True)]
    all_to_all x3 -> x4, waiting for transfers between devices: 39.9 us -> 67.8 us  [swap(): lax.all_to_all(matrix, 'head', split_axis=0, concat_axis=0, tiled=True)]
    all_to_all x3 -> x4, starting transfers between devices: 13.6 us -> 18.6 us  [swap(): lax.all_to_all(matrix, 'head', split_axis=0, concat_axis=0, tiled=True)]
    pallas_call x9 -> x11, Pallas kernels: 27.8 us -> 32.3 us  [call(): pl.pallas_call(body, out_shape=outs, in_specs=smem_specs(len(scalars)) +...]
    unnamed x17 -> x27, local copies, waits for them, and re-layouts: 0.89 us -> 4.59 us
  transfers between devices with their start and end apart: 11 -> 12, of which waited for: 7 -> 8; matrix products, arithmetic and copies ran while one was open for 3% -> 3% of each run, Pallas kernels for 5% -> 7%
where the time goes in v3:
time: 158 us; the launch traced here: 157 us
  waiting for transfers between devices  88 us (56%)
  Pallas kernels  32.3 us (20%)
  starting transfers between devices  27.1 us (17%)
  local copies, waits for them, and re-layouts  8.73 us (6%)
    all_to_all x4, waiting for transfers between devices, swap(): lax.all_to_all(matrix, 'head', split_axis=0, concat_axis=0, tiled=True)  67.8 us
    pallas_call x11, Pallas kernels, call(): pl.pallas_call(body, out_shape=outs, in_specs=smem_specs(len(scalars)) +...  32.3 us
    all_to_all x4, starting transfers between devices, swap(): lax.all_to_all(matrix, 'head', split_axis=0, concat_axis=0, tiled=True)  18.6 us
    ppermute x4, waiting for transfers between devices, permute_back(): return lax.ppermute(value, 'dom', [(d, p) for p, d in pairs])  17.5 us
    unnamed x27, local copies, waits for them, and re-layouts  4.59 us
    ppermute x4, starting transfers between devices, permute_back(): return lax.ppermute(value, 'dom', [(d, p) for p, d in pairs])  4.42 us
    ppermute x4, starting transfers between devices, permute(): return lax.ppermute(value, 'dom', pairs)  4.07 us
  transfers between devices with their start and end apart: 12, of which 8 were waited for; matrix products, arithmetic and copies ran while one was open for 3% of the time, Pallas kernels for 7%

profile of v3, /device:TPU:4, one launch (start us, length us, event | category | flops | bytes accessed | tf_op | source)
XLA Modules:
  0.0 157.0 jit_solution(9309695122450391974)
XLA Ops:
  0.6 2.5 %pack.2 = bf16[4,144,1024]{2,1,0:T(8,128)(2,1)} custom-call(bf16[144,2048]{1,0:T(8,128)(2,1)} %refs_0_.6, bf16[144,2048]{1,0:T(8,128)(2,1)} %refs_1_.2), custom_call_target="tpu_custom_call" | custom-call | flops 1150000000 | tf_op jit(solution)/shard_map/pack/pallas_call | solution.py:338
  3.2 0.0 copy-start.10
  3.2 5.0 %all-to-all-start.1 = ((bf16[4,144,1024]{2,1,0:T(8,128)(2,1)}), bf16[4,144,1024]{2,1,0:T(8,128)(2,1)S(1)}, u32[]{:S(2)}, u32[]{:S(2)}) async-start(bf16[4,144,1024]{2,1,0:T(8,128)(2,1)} %pack.2), calls=%async_computation.1 | async-start | bytes 2359296 | tf_op jit(solution)/shard_map/all_to_all | solution.py:363
  8.2 1.3 slice.8.refs_2_
  9.5 1.4 copy.14.refs_4_
  10.9 1.3 slice.9.refs_3_
  12.2 2.5 %pack.3 = bf16[4,144,1024]{2,1,0:T(8,128)(2,1)} custom-call(bf16[144,2048]{1,0:T(8,128)(2,1)} %refs_0_.7, bf16[144,2048]{1,0:T(8,128)(2,1)} %refs_1_.3, bf16[1,16,128]{2,1,0:T(8,128)(2,1)} %slice.8.refs_2_, f32[1,16,128]{2,1,0:T(8,128)} %slice.9.refs_3_), custom_call_target="tpu_custom_call" | custom-call | flops 1150000000 | tf_op jit(solution)/shard_map/pack/pallas_call | solution.py:338
  14.7 0.0 copy-start.12
  14.7 0.0 copy-start.2
  14.7 22.0 %all-to-all-done.1 = bf16[4,144,1024]{2,1,0:T(8,128)(2,1)S(1)} async-done(((bf16[4,144,1024]{2,1,0:T(8,128)(2,1)}), bf16[4,144,1024]{2,1,0:T(8,128)(2,1)S(1)}, u32[]{:S(2)}, u32[]{:S(2)}) %all-to-all-start.1) | async-done | bytes 1179680 | tf_op jit(solution)/shard_map/all_to_all | solution.py:363
  36.7 3.5 %all-to-all-start = ((bf16[4,144,1024]{2,1,0:T(8,128)(2,1)}), bf16[4,144,1024]{2,1,0:T(8,128)(2,1)S(1)}, u32[]{:S(2)}, u32[]{:S(2)}) async-start(bf16[4,144,1024]{2,1,0:T(8,128)(2,1)} %pack.3), calls=%async_computation | async-start | bytes 2359296 | tf_op jit(solution)/shard_map/all_to_all | solution.py:363
  40.3 0.1 copy.15
  40.4 0.1 reshape.39.refs_1_
  40.4 1.0 lend_corners.1
  41.4 0.0 copy-start.11
  41.5 0.0 copy-start.9
  41.5 0.1 collective-permute-start
  41.5 1.5 collective-permute-done.refs_3_
  43.1 1.8 %lend_edges.1 = (bf16[192,1024]{1,0:T(8,128)(2,1)}, bf16[256,1024]{1,0:T(8,128)(2,1)}, bf16[256,1024]{1,0:T(8,128)(2,1)}) custom-call(s32[8,49]{1,0:T(8,128)S(1)} %copy-done.2, s32[24]{0:T(128)S(1)} %reshape.39.refs_1_, bf16[576,1024]{1,0:T(8,128)(2,1)S(1)} %bitcast.11, bf16[128,1024]{1,0:T(8,128)(2,1)S(1)} %collective-permute-done.refs_3_), custom_call_target="tpu_custom_call" | custom-call | flops 1150000000 | tf_op jit(solution)/shard_map/lend_edges/pallas_call | solution.py:338
  44.9 1.6 collective-permute-start.2
  46.4 2.4 %collective-permute-start.3 = (bf16[256,1024]{1,0:T(8,128)(2,1)}, bf16[256,1024]{1,0:T(8,128)(2,1)S(1)}, u32[]{:S(2)}, u32[]{:S(2)}) collective-permute-start(bf16[256,1024]{1,0:T(8,128)(2,1)} %get-tuple-element.24), channel_id=1, source_target_pairs={{16,8},{20,12},{8,16},{12,20},{17,9},{21,13},{9,17},{13,21},{18,10... | collective-permute-start | bytes 1572872 | tf_op jit(solution)/shard_map/ppermute | solution.py:376
  48.8 0.1 collective-permute-start.1
  48.9 0.1 reshape.33.refs_1_
  49.0 1.4 place.1
  50.4 17.9 %all-to-all-done = bf16[4,144,1024]{2,1,0:T(8,128)(2,1)S(1)} async-done(((bf16[4,144,1024]{2,1,0:T(8,128)(2,1)}), bf16[4,144,1024]{2,1,0:T(8,128)(2,1)S(1)}, u32[]{:S(2)}, u32[]{:S(2)}) %all-to-all-start) | async-done | bytes 1179680 | tf_op jit(solution)/shard_map/all_to_all | solution.py:363
  68.3 0.0 collective-permute-done.2.refs_6_
  68.3 0.0 copy-start.3
  68.3 0.8 copy-done.3
  69.1 1.2 collective-permute-done.3.refs_7_
  70.3 0.8 copy-done.5
  71.1 1.0 copy-done.4
  72.1 1.0 copy-done.6
  73.2 7.8 %attend.2 = (f32[576,512]{1,0:T(8,128)S(1)}, bf16[576,256]{1,0:T(8,128)(2,1)S(1)}, bf16[192,512]{1,0:T(8,128)(2,1)S(1)}, bf16[256,512]{1,0:T(8,128)(2,1)S(1)}, bf16[256,512]{1,0:T(8,128)(2,1)S(1)}) custom-call(s32[81]{0:T(128)S(1)} %get-tuple-element.20.refs_0_, s32[11]{0:T(128)S(1)} %get-tuple-element.21.refs_1_, bf16[576,1024]{1,0:T(8,128)(2,1)S(1)} %bitcast.14, ...), custom_call_target="tpu_custom_call" | custom-call | flops 9200000000 | tf_op jit(solution)/shard_map/attend/pallas_call | solution.py:338
  81.0 9.6 %attend.3 = (f32[576,512]{1,0:T(8,128)S(1)}, bf16[576,512]{1,0:T(8,128)(2,1)}, bf16[192,1024]{1,0:T(8,128)(2,1)S(1)}, bf16[256,1024]{1,0:T(8,128)(2,1)}, bf16[256,1024]{1,0:T(8,128)(2,1)}) custom-call(s32[81]{0:T(128)S(1)} %get-tuple-element.20.refs_0_, s32[11]{0:T(128)S(1)} %get-tuple-element.21.refs_1_, bf16[576,1024]{1,0:T(8,128)(2,1)} %bitcast.15, ...), custom_call_target="tpu_custom_call" | custom-call | flops 9200000000 | tf_op jit(solution)/shard_map/attend/pallas_call | solution.py:338
  90.6 0.7 copy-done.8
  91.3 0.3 collective-permute-start.5
  91.7 4.0 %collective-permute-start.6 = (bf16[256,1024]{1,0:T(8,128)(2,1)}, bf16[256,1024]{1,0:T(8,128)(2,1)}, u32[]{:S(2)}, u32[]{:S(2)}) collective-permute-start(bf16[256,1024]{1,0:T(8,128)(2,1)} %get-tuple-element.34), channel_id=1, source_target_pairs={{8,16},{12,20},{16,8},{20,12},{9,17},{13,21},{17,9},{21,13},{10,18... | collective-permute-start | bytes 1572872 | tf_op jit(solution)/shard_map/ppermute | solution.py:379
  95.7 5.1 %all-to-all-start.2 = ((bf16[4,144,512]{2,1,0:T(8,128)(2,1)}), bf16[4,144,512]{2,1,0:T(8,128)(2,1)S(1)}, u32[]{:S(2)}, u32[]{:S(2)}) async-start(bf16[4,144,512]{2,1,0:T(8,128)(2,1)} %bitcast.6), calls=%async_computation.2 | async-start | bytes 1179648 | tf_op jit(solution)/shard_map/all_to_all | solution.py:363
  100.7 3.9 %collective-permute-done.5.refs_0_.refs_5_ = bf16[256,1024]{1,0:T(8,128)(2,1)S(1)} collective-permute-done((bf16[256,1024]{1,0:T(8,128)(2,1)}, bf16[256,1024]{1,0:T(8,128)(2,1)S(1)}, u32[]{:S(2)}, u32[]{:S(2)}) %collective-permute-start.5) | collective-permute-done | bytes 524320 | tf_op jit(solution)/shard_map/ppermute | solution.py:379
  104.7 12.0 %collective-permute-done.6.refs_1_.refs_6_ = bf16[256,1024]{1,0:T(8,128)(2,1)} collective-permute-done((bf16[256,1024]{1,0:T(8,128)(2,1)}, bf16[256,1024]{1,0:T(8,128)(2,1)}, u32[]{:S(2)}, u32[]{:S(2)}) %collective-permute-start.6) | collective-permute-done | bytes 524320 | tf_op jit(solution)/shard_map/ppermute | solution.py:379
  116.7 1.1 forward.1
  117.8 0.1 collective-permute-start.7
  117.9 1.5 collective-permute-done.7.refs_7_
  119.4 2.6 %settle.1 = bf16[576,1024]{1,0:T(8,128)(2,1)} custom-call(s32[8,49]{1,0:T(8,128)S(1)} %copy-done.2, s32[24]{0:T(128)S(1)} %reshape.39.refs_1_, f32[576,512]{1,0:T(8,128)S(1)} %get-tuple-element.30.refs_2_, f32[576,512]{1,0:T(8,128)S(1)} %get-tuple-element.31.refs_3_, bf16[192,1024]{1,0:T(8,128)(2,1)S(1)} %collective-permute-done.4.refs_4_, ...), custom_call_target="tpu_custom_call" | custom-call | flops 1150000000 | tf_op jit(solution)/shard_map/settle/pallas_call | solution.py:338
  122.0 5.1 %all-to-all-start.3 = ((bf16[4,144,1024]{2,1,0:T(8,128)(2,1)}), bf16[4,144,1024]{2,1,0:T(8,128)(2,1)S(1)}, u32[]{:S(2)}, u32[]{:S(2)}) async-start(bf16[4,144,1024]{2,1,0:T(8,128)(2,1)} %bitcast.7), calls=%async_computation.3 | async-start | bytes 2359296 | tf_op jit(solution)/shard_map/all_to_all | solution.py:363
  127.0 0.9 unpack.2
  127.9 28.0 %all-to-all-done.3.refs_0_ = bf16[4,144,1024]{2,1,0:T(8,128)(2,1)S(1)} async-done(((bf16[4,144,1024]{2,1,0:T(8,128)(2,1)}), bf16[4,144,1024]{2,1,0:T(8,128)(2,1)S(1)}, u32[]{:S(2)}, u32[]{:S(2)}) %all-to-all-start.3) | async-done | bytes 1179680 | tf_op jit(solution)/shard_map/all_to_all | solution.py:363
  155.9 1.2 unpack.3
  (19 shorter events, 0.0 us)
Async XLA Ops:
  3.2 6.3 %copy-start.10 = (f32[8,64,576]{2,1,0:T(8,128)S(1)}, f32[8,64,576]{2,1,0:T(8,128)}, u32[]{:S(2)}) copy-start(f32[8,64,576]{2,1,0:T(8,128)} %param.13) | copy-start | bytes 3538948
  3.2 33.5 %all-to-all-start.1 = ((bf16[4,144,1024]{2,1,0:T(8,128)(2,1)}), bf16[4,144,1024]{2,1,0:T(8,128)(2,1)S(1)}, u32[]{:S(2)}, u32[]{:S(2)}) async-start(bf16[4,144,1024]{2,1,0:T(8,128)(2,1)} %pack.2), calls=%async_computation.1 | async-start | bytes 2359296 | tf_op jit(solution)/shard_map/all_to_all | solution.py:363
  14.7 25.6 %copy-start.12 = (s32[1,8,3]{1,0,2:T(1,128)S(1)}, s32[1,8,3]{1,0,2:T(1,128)}, u32[]{:S(2)}) copy-start(s32[1,8,3]{1,0,2:T(1,128)} %param.15) | copy-start | bytes 292
  14.7 25.7 %copy-start.2 = (s32[8,49]{1,0:T(8,128)S(1)}, s32[8,49]{1,0:T(8,128)}, u32[]{:S(2)}) copy-start(s32[8,49]{1,0:T(8,128)} %constant.2.clone.refs_0_) | copy-start | bytes 4708
  36.7 34.4 %copy-start = (bf16[4,144,1024]{2,1,0:T(8,128)(2,1)}, bf16[4,144,1024]{2,1,0:T(8,128)(2,1)S(1)}, u32[]{:S(2)}) copy-start(bf16[4,144,1024]{2,1,0:T(8,128)(2,1)S(1)} %all-to-all-done.1) | copy-start | bytes 3538948
  36.7 31.5 %all-to-all-start = ((bf16[4,144,1024]{2,1,0:T(8,128)(2,1)}), bf16[4,144,1024]{2,1,0:T(8,128)(2,1)S(1)}, u32[]{:S(2)}, u32[]{:S(2)}) async-start(bf16[4,144,1024]{2,1,0:T(8,128)(2,1)} %pack.3), calls=%async_computation | async-start | bytes 2359296 | tf_op jit(solution)/shard_map/all_to_all | solution.py:363
  41.4 7.5 %copy-start.11 = (s32[9,9]{1,0:T(8,128)S(1)}, s32[9,9]{1,0:T(8,128)}, u32[]{:S(2)}) copy-start(s32[9,9]{1,0:T(8,128)} %param.14) | copy-start | bytes 976
  41.5 7.5 %copy-start.9 = (s32[1,8]{1,0:T(1,128)S(1)}, s32[1,8]{1,0:T(1,128)}, u32[]{:S(2)}) copy-start(s32[1,8]{1,0:T(1,128)} %param.16) | copy-start | bytes 100
  41.5 1.6 %collective-permute-start = (bf16[128,1024]{1,0:T(8,128)(2,1)S(1)}, bf16[128,1024]{1,0:T(8,128)(2,1)S(1)}, u32[]{:S(2)}, u32[]{:S(2)}) collective-permute-start(bf16[128,1024]{1,0:T(8,128)(2,1)S(1)} %lend_corners.1), channel_id=1, source_target_pairs={{0,4},{8,12},{16,20},{24,28},{4,0},{12,8},{20,16},{28,24},{1,5},{9... | collective-permute-start | bytes 786440 | tf_op jit(solution)/shard_map/ppermute | solution.py:376
  44.9 23.4 %collective-permute-start.2 = (bf16[256,1024]{1,0:T(8,128)(2,1)}, bf16[256,1024]{1,0:T(8,128)(2,1)S(1)}, u32[]{:S(2)}, u32[]{:S(2)}) collective-permute-start(bf16[256,1024]{1,0:T(8,128)(2,1)} %get-tuple-element.23), channel_id=1, source_target_pairs={{8,0},{12,4},{0,8},{4,12},{24,16},{28,20},{16,24},{20,28},{9,1},{1... | collective-permute-start | bytes 1572872 | tf_op jit(solution)/shard_map/ppermute | solution.py:376
  46.4 23.9 %collective-permute-start.3 = (bf16[256,1024]{1,0:T(8,128)(2,1)}, bf16[256,1024]{1,0:T(8,128)(2,1)S(1)}, u32[]{:S(2)}, u32[]{:S(2)}) collective-permute-start(bf16[256,1024]{1,0:T(8,128)(2,1)} %get-tuple-element.24), channel_id=1, source_target_pairs={{16,8},{20,12},{8,16},{12,20},{17,9},{21,13},{9,17},{13,21},{18,10... | collective-permute-start | bytes 1572872 | tf_op jit(solution)/shard_map/ppermute | solution.py:376
  48.8 19.5 %collective-permute-start.1 = (bf16[192,1024]{1,0:T(8,128)(2,1)}, bf16[192,1024]{1,0:T(8,128)(2,1)}, u32[]{:S(2)}, u32[]{:S(2)}) collective-permute-start(bf16[192,1024]{1,0:T(8,128)(2,1)} %get-tuple-element.22), channel_id=1, source_target_pairs={{0,4},{8,12},{16,20},{24,28},{4,0},{12,8},{20,16},{28,24},{1,5},{9... | collective-permute-start | bytes 1179656 | tf_op jit(solution)/shard_map/ppermute | solution.py:376
  68.3 12.7 %copy-start.1 = (bf16[4,144,1024]{2,1,0:T(8,128)(2,1)}, bf16[4,144,1024]{2,1,0:T(8,128)(2,1)S(1)}, u32[]{:S(2)}) copy-start(bf16[4,144,1024]{2,1,0:T(8,128)(2,1)S(1)} %all-to-all-done) | copy-start | bytes 3538948
  68.3 0.9 copy-start.3
  70.3 0.8 copy-start.5
  71.1 1.0 copy-start.4
  72.1 1.0 copy-start.6
  73.2 7.8 %copy-start.7 = (bf16[256,1024]{1,0:T(8,128)(2,1)S(1)}, bf16[256,1024]{1,0:T(8,128)(2,1)}, u32[]{:S(2)}) copy-start(bf16[256,1024]{1,0:T(8,128)(2,1)} %copy-done.5) | copy-start | bytes 1572868
  90.6 0.7 copy-start.8
  91.3 13.3 %collective-permute-start.5 = (bf16[256,1024]{1,0:T(8,128)(2,1)}, bf16[256,1024]{1,0:T(8,128)(2,1)S(1)}, u32[]{:S(2)}, u32[]{:S(2)}) collective-permute-start(bf16[256,1024]{1,0:T(8,128)(2,1)} %get-tuple-element.33), channel_id=1, source_target_pairs={{0,8},{4,12},{8,0},{12,4},{16,24},{20,28},{24,16},{28,20},{1,9},{5... | collective-permute-start | bytes 1572872 | tf_op jit(solution)/shard_map/ppermute | solution.py:379
  91.7 25.1 %collective-permute-start.6 = (bf16[256,1024]{1,0:T(8,128)(2,1)}, bf16[256,1024]{1,0:T(8,128)(2,1)}, u32[]{:S(2)}, u32[]{:S(2)}) collective-permute-start(bf16[256,1024]{1,0:T(8,128)(2,1)} %get-tuple-element.34), channel_id=1, source_target_pairs={{8,16},{12,20},{16,8},{20,12},{9,17},{13,21},{17,9},{21,13},{10,18... | collective-permute-start | bytes 1572872 | tf_op jit(solution)/shard_map/ppermute | solution.py:379
  95.7 26.3 %all-to-all-start.2 = ((bf16[4,144,512]{2,1,0:T(8,128)(2,1)}), bf16[4,144,512]{2,1,0:T(8,128)(2,1)S(1)}, u32[]{:S(2)}, u32[]{:S(2)}) async-start(bf16[4,144,512]{2,1,0:T(8,128)(2,1)} %bitcast.6), calls=%async_computation.2 | async-start | bytes 1179648 | tf_op jit(solution)/shard_map/all_to_all | solution.py:363
  100.7 17.1 %collective-permute-start.4 = (bf16[192,1024]{1,0:T(8,128)(2,1)}, bf16[192,1024]{1,0:T(8,128)(2,1)S(1)}, u32[]{:S(2)}, u32[]{:S(2)}) collective-permute-start(bf16[192,1024]{1,0:T(8,128)(2,1)} %copy-done.8), channel_id=1, source_target_pairs={{4,0},{12,8},{20,16},{28,24},{0,4},{8,12},{16,20},{24,28},{5,1},{1... | collective-permute-start | bytes 1179656 | tf_op jit(solution)/shard_map/ppermute | solution.py:379
  117.8 1.6 %collective-permute-start.7 = (bf16[128,1024]{1,0:T(8,128)(2,1)S(1)}, bf16[128,1024]{1,0:T(8,128)(2,1)S(1)}, u32[]{:S(2)}, u32[]{:S(2)}) collective-permute-start(bf16[128,1024]{1,0:T(8,128)(2,1)S(1)} %forward.1), channel_id=1, source_target_pairs={{4,0},{12,8},{20,16},{28,24},{0,4},{8,12},{16,20},{24,28},{5,1},{1... | collective-permute-start | bytes 786440 | tf_op jit(solution)/shard_map/ppermute | solution.py:379
  122.0 33.9 %all-to-all-start.3 = ((bf16[4,144,1024]{2,1,0:T(8,128)(2,1)}), bf16[4,144,1024]{2,1,0:T(8,128)(2,1)S(1)}, u32[]{:S(2)}, u32[]{:S(2)}) async-start(bf16[4,144,1024]{2,1,0:T(8,128)(2,1)} %bitcast.7), calls=%async_computation.3 | async-start | bytes 2359296 | tf_op jit(solution)/shard_map/all_to_all | solution.py:363

commit v4 on v2

--- a/solution.py
+++ b/solution.py
@@ -185,7 +185,9 @@
     out_ref, total = refs[-2:]
     sides, rises = refs[:plan.sides], refs[plan.sides:plan.sides + 2]
     corners = refs[plan.sides + 2:-2]
-    total[...] = own_ref[...]
+    columns = own_ref.shape[2]
+    for part in range(own_ref.shape[0]):
+        total[:, part * columns:(part + 1) * columns] = own_ref[part]
 
     def add(block, ref, c):
         total[block_rows(block), :] += ref[rows_of(c), :].astype(jnp.float32)
@@ -210,7 +212,8 @@
     groups = len(plan.shapes)
     arrived = refs[:groups]
     dq_ref, own_ref, *leaving = refs[groups:2 * groups + 2]
-    ext, acc, qg, dq, win, work, probs_ref, dscores_ref = refs[2 * groups + 2:]
+    ext, acc, qg, dq, bias, win, work, probs_ref, dscores_ref = refs[2 * groups + 2:2 * groups + 11]
+    turned_back, (in_sems, out_sems, leave_sems) = refs[2 * groups + 11:-3], refs[-3:]
     width = dq.shape[2]
     heads = width // HD
     scale = HD ** -0.5
@@ -222,9 +225,16 @@
     def turned(i, c, back):
         return turn_matrix(turns_ref[plan.starts[i] - QB_DOM + c], back)
 
-    for part, pair in enumerate(pairs):
-        qg[part] = qg_ref[:, pair]
-        ext[part, :QB_DOM * BT, :] = kv_ref[:, pair]
+    def copies(part, moves, sems):
+        return [pltpu.make_async_copy(source, target, sems.at[part, n]) for n, (source, target) in enumerate(moves)]
+
+    loads = [copies(part, [(kv_ref.at[:, pair], ext.at[part, :QB_DOM * BT, :]), (qg_ref.at[:, pair], qg.at[part]),
+                           (bias_ref.at[part], bias.at[part])], in_sems) for part, pair in enumerate(pairs)]
+    stores = [copies(part, [(acc.at[part, :QB_DOM * BT, :], own_ref.at[part]),
+                            (dq.at[part], dq_ref.at[:, part * width:(part + 1) * width])], out_sems)
+              for part in range(parts)]
+    for copy in sum(loads, []):
+        copy.start()
     for i, count in enumerate(plan.shapes):
         for c in range(count):
             if c == 0 or c >= CAP:
@@ -247,7 +257,7 @@
             win[even, rows_of(j), :] = ext[part, places[b * WIN + j], :]
         query = spread(qg[part, rows_of(b), keys] * jnp.bfloat16(scale))
         grad = spread(qg[part, rows_of(b), values])
-        work[even, 0] = dot(win[even, :, keys], query, (1, 1)) + bias_ref[part]
+        work[even, 0] = dot(win[even, :, keys], query, (1, 1)) + bias[part]
         work[even, 1] = dot(win[even, :, values], grad, (1, 1))
         return query, grad
 
@@ -286,26 +296,37 @@
             acc[part, places[b * WIN + j], keys] += grad_k[rows_of(j)]
             acc[part, places[b * WIN + j], values] += grad_v[rows_of(j)]
 
+    def only(part, these, act):
+        for n in range(parts):
+            @pl.when(part == n)
+            def _():
+                for copy in these[n]:
+                    act(copy)
+
     def one_part(part, carry):
+        only(part, loads, lambda copy: copy.wait())
         here = products(part, 0)
         for b in range(QB_DOM):
             following = products(part, b + 1) if b + 1 < QB_DOM else None
             softmax(b)
             gradients(part, b, *here)
             here = following
+        only(part, stores, lambda copy: copy.start())
         return carry
 
     lax.fori_loop(0, parts, one_part, 0)
-    for part, pair in enumerate(pairs):
-        own_ref[:, pair] = acc[part, :QB_DOM * BT, :]
-        dq_ref[:, part * width:(part + 1) * width] = dq[part]
+    leaves = []
     for i, count in enumerate(plan.shapes):
         for c in range(count):
             if c == 0 or c >= CAP:
                 turn = turned(i, c, True)
             for part, pair in enumerate(pairs):
                 slot = acc[part, rows_of(plan.starts[i] + c), :].astype(jnp.bfloat16)
-                leaving[i][rows_of(c), pair] = dot(turn, slot, (1, 0)).astype(jnp.bfloat16)
+                turned_back[i][rows_of(c), pair] = dot(turn, slot, (1, 0)).astype(jnp.bfloat16)
+        leaves.append(pltpu.make_async_copy(turned_back[i], leaving[i], leave_sems.at[i]))
+        leaves[-1].start()
+    for copy in sum(stores, []) + leaves:
+        copy.wait()
 
 
 def smem_specs(count):
@@ -332,7 +353,7 @@
     return pl.CostEstimate(flops=int(microseconds * 1.15e9), bytes_accessed=0, transcendentals=0)
 
 
-def call(kernel, name, scalars, arrays, outs, after=(), in_place=False, out_specs=None, takes=1.0, limit=VMEM_LIMIT, **more):
+def call(kernel, name, scalars, arrays, outs, after=(), in_place=False, in_specs=None, out_specs=None, takes=1.0, limit=VMEM_LIMIT, **more):
     after = [x[tuple(slice(0, n) for n in (1,) * (x.ndim - 2) + (16, 128))] for x in after]
     taken = len(scalars) + len(arrays)
 
@@ -342,7 +363,8 @@
     return pl.pallas_call(
         body,
         out_shape=outs,
-        in_specs=smem_specs(len(scalars)) + (any_specs if in_place else vmem_specs)(len(arrays)) + any_specs(len(after)),
+        in_specs=smem_specs(len(scalars)) + (in_specs or (any_specs if in_place else vmem_specs)(len(arrays)))
+        + any_specs(len(after)),
         out_specs=out_specs or vmem_specs(len(outs)),
         compiler_params=params(limit),
         cost_estimate=busy(takes),
@@ -405,17 +427,23 @@
 
     grad_q, own, *leaving = call(
         functools.partial(attend_kernel, plan, parts), "attend", [places, turned], [qg, kv, bias, *arrived],
-        [bf16(tokens_dom, width), jax.ShapeDtypeStruct((tokens_dom, 2 * width), jnp.float32)] + block_shapes,
+        [bf16(tokens_dom, width), jax.ShapeDtypeStruct((parts, tokens_dom, 2 * part_width), jnp.float32)] + block_shapes,
+        in_specs=any_specs(3) + vmem_specs(len(arrived)), out_specs=any_specs(2 + len(block_shapes)),
         takes=15.0,
         scratch_shapes=[
             pltpu.VMEM((parts, plan.slots * BT, 2 * part_width), jnp.bfloat16),
             pltpu.VMEM((parts, plan.slots * BT, 2 * part_width), jnp.float32),
             pltpu.VMEM((parts, tokens_dom, 2 * part_width), jnp.bfloat16),
             pltpu.VMEM((parts, tokens_dom, part_width), jnp.bfloat16),
+            pltpu.VMEM((parts, WINK, part_width), jnp.float32),
             pltpu.VMEM((2, WINK, 2 * part_width), jnp.bfloat16),
             pltpu.VMEM((2, 2, WINK, part_width), jnp.float32),
             pltpu.VMEM((2, WINK, part_width), jnp.bfloat16),
             pltpu.VMEM((2, WINK, part_width), jnp.bfloat16),
+            *[pltpu.VMEM(shape.shape, jnp.bfloat16) for shape in block_shapes],
+            pltpu.SemaphoreType.DMA((parts, 3)),
+            pltpu.SemaphoreType.DMA((parts, 2)),
+            pltpu.SemaphoreType.DMA((len(block_shapes),)),
         ],
     )
     rises = [permute_back(x, pairs) for x, pairs in zip(leaving[sides:], plan.rise_pairs)]

time: 151 us -> 150 us (level)
  no operation moved by 1% of the time
where the time goes in v4:
time: 150 us
  waiting for transfers between devices  60.8 us (41%)
  blocking collectives  33.7 us (22%)
  Pallas kernels  27.1 us (18%)
  starting transfers between devices  22.2 us (15%)
  local copies, waits for them, and re-layouts  5.02 us (3%)
    all_to_all x3, waiting for transfers between devices, swap(): lax.all_to_all(matrix, 'head', split_axis=0, concat_axis=0, tiled=True)  39.9 us
    all_to_all x1, blocking collectives, swap(): lax.all_to_all(matrix, 'head', split_axis=0, concat_axis=0, tiled=True)  33.7 us
    pallas_call x9, Pallas kernels, call(): pl.pallas_call(body, out_shape=outs, in_specs=smem_specs(len(scalars)) +...  27.1 us
    ppermute x4, waiting for transfers between devices, permute_back(): return lax.ppermute(value, 'dom', [(d, p) for p, d in pairs])  17.2 us
    all_to_all x3, starting transfers between devices, swap(): lax.all_to_all(matrix, 'head', split_axis=0, concat_axis=0, tiled=True)  13.6 us
    ppermute x4, starting transfers between devices, permute_back(): return lax.ppermute(value, 'dom', [(d, p) for p, d in pairs])  4.55 us
    ppermute x4, starting transfers between devices, permute(): return lax.ppermute(value, 'dom', pairs)  4.07 us
    ppermute x4, waiting for transfers between devices, permute(): return lax.ppermute(value, 'dom', pairs)  3.65 us
  transfers between devices with their start and end apart: 11, of which 7 were waited for; matrix products, arithmetic and copies ran while one was open for 3% of the time, Pallas kernels for 5%

profile of v4, /device:TPU:4, one launch (start us, length us, event | category | flops | bytes accessed | tf_op | source)
XLA Modules:
  0.0 149.6 jit_solution(16703408409013288503)
XLA Ops:
  0.6 2.5 %pack.2 = bf16[4,144,1024]{2,1,0:T(8,128)(2,1)} custom-call(bf16[144,2048]{1,0:T(8,128)(2,1)} %refs_0_.6, bf16[144,2048]{1,0:T(8,128)(2,1)} %refs_1_.2), custom_call_target="tpu_custom_call" | custom-call | flops 1150000000 | tf_op jit(solution)/shard_map/pack/pallas_call | solution.py:363
  3.2 0.0 copy-start.5
  3.2 5.0 %all-to-all-start.1 = ((bf16[4,144,1024]{2,1,0:T(8,128)(2,1)}), bf16[4,144,1024]{2,1,0:T(8,128)(2,1)S(1)}, u32[]{:S(2)}, u32[]{:S(2)}) async-start(bf16[4,144,1024]{2,1,0:T(8,128)(2,1)} %pack.2), calls=%async_computation.1 | async-start | bytes 2359296 | tf_op jit(solution)/shard_map/all_to_all | solution.py:389
  8.2 1.3 slice.8.refs_2_
  9.4 0.0 copy-done.5
  9.5 1.4 copy.14.refs_4_
  10.9 1.3 slice.9.refs_3_
  12.2 2.5 %pack.3 = bf16[4,144,1024]{2,1,0:T(8,128)(2,1)} custom-call(bf16[144,2048]{1,0:T(8,128)(2,1)} %refs_0_.7, bf16[144,2048]{1,0:T(8,128)(2,1)} %refs_1_.3, bf16[1,16,128]{2,1,0:T(8,128)(2,1)} %slice.8.refs_2_, f32[1,16,128]{2,1,0:T(8,128)} %slice.9.refs_3_), custom_call_target="tpu_custom_call" | custom-call | flops 1150000000 | tf_op jit(solution)/shard_map/pack/pallas_call | solution.py:363
  14.7 0.0 copy-start.7
  14.7 0.0 copy-start.1
  14.7 22.0 %all-to-all-done.1 = bf16[4,144,1024]{2,1,0:T(8,128)(2,1)S(1)} async-done(((bf16[4,144,1024]{2,1,0:T(8,128)(2,1)}), bf16[4,144,1024]{2,1,0:T(8,128)(2,1)S(1)}, u32[]{:S(2)}, u32[]{:S(2)}) %all-to-all-start.1) | async-done | bytes 1179680 | tf_op jit(solution)/shard_map/all_to_all | solution.py:389
  36.7 3.5 %all-to-all-start = ((bf16[4,144,1024]{2,1,0:T(8,128)(2,1)}), bf16[4,144,1024]{2,1,0:T(8,128)(2,1)S(1)}, u32[]{:S(2)}, u32[]{:S(2)}) async-start(bf16[4,144,1024]{2,1,0:T(8,128)(2,1)} %pack.3), calls=%async_computation | async-start | bytes 2359296 | tf_op jit(solution)/shard_map/all_to_all | solution.py:389
  40.3 0.0 copy-done.7
  40.3 0.1 copy.15
  40.3 0.1 reshape.39.refs_1_
  40.4 0.0 copy-done.1
  40.4 1.0 lend_corners.1
  41.4 0.0 copy-start.6
  41.4 0.0 copy-start.4
  41.5 0.1 collective-permute-start
  41.5 1.5 %collective-permute-done.refs_3_ = bf16[128,1024]{1,0:T(8,128)(2,1)S(1)} collective-permute-done((bf16[128,1024]{1,0:T(8,128)(2,1)S(1)}, bf16[128,1024]{1,0:T(8,128)(2,1)S(1)}, u32[]{:S(2)}, u32[]{:S(2)}) %collective-permute-start) | collective-permute-done | bytes 262176 | tf_op jit(solution)/shard_map/ppermute | solution.py:402
  43.1 1.8 %lend_edges.1 = (bf16[192,1024]{1,0:T(8,128)(2,1)}, bf16[256,1024]{1,0:T(8,128)(2,1)}, bf16[256,1024]{1,0:T(8,128)(2,1)}) custom-call(s32[8,49]{1,0:T(8,128)S(1)} %copy-done.1, s32[24]{0:T(128)S(1)} %reshape.39.refs_1_, bf16[576,1024]{1,0:T(8,128)(2,1)S(1)} %bitcast.12, bf16[128,1024]{1,0:T(8,128)(2,1)S(1)} %collective-permute-done.refs_3_), custom_call_target="tpu_custom_call" | custom-call | flops 1150000000 | tf_op jit(solution)/shard_map/lend_edges/pallas_call | solution.py:363
  44.9 1.6 %collective-permute-start.2 = (bf16[256,1024]{1,0:T(8,128)(2,1)}, bf16[256,1024]{1,0:T(8,128)(2,1)S(1)}, u32[]{:S(2)}, u32[]{:S(2)}) collective-permute-start(bf16[256,1024]{1,0:T(8,128)(2,1)} %get-tuple-element.16), channel_id=1, source_target_pairs={{8,0},{12,4},{0,8},{4,12},{24,16},{28,20},{16,24},{20,28},{9,1},{1... | collective-permute-start | bytes 1572872 | tf_op jit(solution)/shard_map/ppermute | solution.py:402
  46.4 2.4 %collective-permute-start.3 = (bf16[256,1024]{1,0:T(8,128)(2,1)}, bf16[256,1024]{1,0:T(8,128)(2,1)}, u32[]{:S(2)}, u32[]{:S(2)}) collective-permute-start(bf16[256,1024]{1,0:T(8,128)(2,1)} %get-tuple-element.17), channel_id=1, source_target_pairs={{16,8},{20,12},{8,16},{12,20},{17,9},{21,13},{9,17},{13,21},{18,10... | collective-permute-start | bytes 1572872 | tf_op jit(solution)/shard_map/ppermute | solution.py:402
  48.8 0.1 collective-permute-start.1
  48.9 0.0 copy-done.6
  48.9 0.1 reshape.33.refs_1_
  49.0 0.0 copy-done.4
  49.0 1.4 place.1
  50.4 17.9 %all-to-all-done = bf16[4,144,1024]{2,1,0:T(8,128)(2,1)S(1)} async-done(((bf16[4,144,1024]{2,1,0:T(8,128)(2,1)}), bf16[4,144,1024]{2,1,0:T(8,128)(2,1)S(1)}, u32[]{:S(2)}, u32[]{:S(2)}) %all-to-all-start) | async-done | bytes 1179680 | tf_op jit(solution)/shard_map/all_to_all | solution.py:389
  68.3 0.0 collective-permute-done.1.refs_5_
  68.3 0.0 collective-permute-done.2.refs_6_
  68.3 2.1 %collective-permute-done.3.refs_7_ = bf16[256,1024]{1,0:T(8,128)(2,1)} collective-permute-done((bf16[256,1024]{1,0:T(8,128)(2,1)}, bf16[256,1024]{1,0:T(8,128)(2,1)}, u32[]{:S(2)}, u32[]{:S(2)}) %collective-permute-start.3) | collective-permute-done | bytes 524320 | tf_op jit(solution)/shard_map/ppermute | solution.py:402
  70.4 15.3 %attend.1 = (bf16[576,512]{1,0:T(8,128)(2,1)}, f32[2,576,512]{2,1,0:T(8,128)}, bf16[192,1024]{1,0:T(8,128)(2,1)S(1)}, bf16[256,1024]{1,0:T(8,128)(2,1)}, bf16[256,1024]{1,0:T(8,128)(2,1)}) custom-call(s32[81]{0:T(128)S(1)} %get-tuple-element.13.refs_0_, s32[11]{0:T(128)S(1)} %get-tuple-element.14.refs_1_, bf16[576,1024]{1,0:T(8,128)(2,1)S(1)} %bitcast.14, ...), custom_call_target="tpu_custom_call" | custom-call | flops 17250000896 | tf_op jit(solution)/shard_map/attend/pallas_call | solution.py:363
  85.7 0.8 copy-done.2
  86.5 0.0 collective-permute-start.5
  86.5 4.5 %collective-permute-start.6 = (bf16[256,1024]{1,0:T(8,128)(2,1)}, bf16[256,1024]{1,0:T(8,128)(2,1)S(1)}, u32[]{:S(2)}, u32[]{:S(2)}) collective-permute-start(bf16[256,1024]{1,0:T(8,128)(2,1)} %get-tuple-element.22), channel_id=1, source_target_pairs={{8,16},{12,20},{16,8},{20,12},{9,17},{13,21},{17,9},{21,13},{10,18... | collective-permute-start | bytes 1572872 | tf_op jit(solution)/shard_map/ppermute | solution.py:405
  91.0 5.1 %all-to-all-start.2 = ((bf16[4,144,512]{2,1,0:T(8,128)(2,1)}), bf16[4,144,512]{2,1,0:T(8,128)(2,1)S(1)}, u32[]{:S(2)}, u32[]{:S(2)}) async-start(bf16[4,144,512]{2,1,0:T(8,128)(2,1)} %bitcast.6), calls=%async_computation.2 | async-start | bytes 1179648 | tf_op jit(solution)/shard_map/all_to_all | solution.py:389
  96.0 0.0 collective-permute-start.4
  96.0 3.8 %collective-permute-done.5.refs_0_.refs_4_ = bf16[256,1024]{1,0:T(8,128)(2,1)S(1)} collective-permute-done((bf16[256,1024]{1,0:T(8,128)(2,1)}, bf16[256,1024]{1,0:T(8,128)(2,1)S(1)}, u32[]{:S(2)}, u32[]{:S(2)}) %collective-permute-start.5) | collective-permute-done | bytes 524320 | tf_op jit(solution)/shard_map/ppermute | solution.py:405
  99.8 11.9 %collective-permute-done.6.refs_1_.refs_5_ = bf16[256,1024]{1,0:T(8,128)(2,1)S(1)} collective-permute-done((bf16[256,1024]{1,0:T(8,128)(2,1)}, bf16[256,1024]{1,0:T(8,128)(2,1)S(1)}, u32[]{:S(2)}, u32[]{:S(2)}) %collective-permute-start.6) | collective-permute-done | bytes 524320 | tf_op jit(solution)/shard_map/ppermute | solution.py:405
  111.8 0.1 collective-permute-start.7
  111.9 0.0 collective-permute-done.4.refs_3_
  111.9 1.5 %collective-permute-done.7.refs_6_ = bf16[128,1024]{1,0:T(8,128)(2,1)S(1)} collective-permute-done((bf16[128,1024]{1,0:T(8,128)(2,1)S(1)}, bf16[128,1024]{1,0:T(8,128)(2,1)S(1)}, u32[]{:S(2)}, u32[]{:S(2)}) %collective-permute-start.7) | collective-permute-done | bytes 262176 | tf_op jit(solution)/shard_map/ppermute | solution.py:405
  113.4 1.1 settle.1
  114.5 0.0 all-to-all-done.2.refs_0_
  114.5 33.7 %all_to_all.20.refs_1_ = bf16[4,144,1024]{2,1,0:T(8,128)(2,1)S(1)} all-to-all(bf16[4,144,1024]{2,1,0:T(8,128)(2,1)S(1)} %bitcast.10), channel_id=1, replica_groups=mesh['dom'=8,'head'=4] {'head'}, dimensions={0} | all-to-all | bytes 2359296 | tf_op jit(solution)/shard_map/all_to_all | solution.py:389
  148.2 1.4 unpack.1
  (6 shorter events, 0.0 us)
Async XLA Ops:
  3.2 6.3 %copy-start.5 = (f32[8,64,576]{2,1,0:T(8,128)S(1)}, f32[8,64,576]{2,1,0:T(8,128)}, u32[]{:S(2)}) copy-start(f32[8,64,576]{2,1,0:T(8,128)} %param.13) | copy-start | bytes 3538948
  3.2 33.5 %all-to-all-start.1 = ((bf16[4,144,1024]{2,1,0:T(8,128)(2,1)}), bf16[4,144,1024]{2,1,0:T(8,128)(2,1)S(1)}, u32[]{:S(2)}, u32[]{:S(2)}) async-start(bf16[4,144,1024]{2,1,0:T(8,128)(2,1)} %pack.2), calls=%async_computation.1 | async-start | bytes 2359296 | tf_op jit(solution)/shard_map/all_to_all | solution.py:389
  14.7 25.6 %copy-start.7 = (s32[1,8,3]{1,0,2:T(1,128)S(1)}, s32[1,8,3]{1,0,2:T(1,128)}, u32[]{:S(2)}) copy-start(s32[1,8,3]{1,0,2:T(1,128)} %param.15) | copy-start | bytes 292
  14.7 25.7 %copy-start.1 = (s32[8,49]{1,0:T(8,128)S(1)}, s32[8,49]{1,0:T(8,128)}, u32[]{:S(2)}) copy-start(s32[8,49]{1,0:T(8,128)} %constant.2.clone.refs_0_) | copy-start | bytes 4708
  36.7 31.5 %all-to-all-start = ((bf16[4,144,1024]{2,1,0:T(8,128)(2,1)}), bf16[4,144,1024]{2,1,0:T(8,128)(2,1)S(1)}, u32[]{:S(2)}, u32[]{:S(2)}) async-start(bf16[4,144,1024]{2,1,0:T(8,128)(2,1)} %pack.3), calls=%async_computation | async-start | bytes 2359296 | tf_op jit(solution)/shard_map/all_to_all | solution.py:389
  41.4 7.5 %copy-start.6 = (s32[9,9]{1,0:T(8,128)S(1)}, s32[9,9]{1,0:T(8,128)}, u32[]{:S(2)}) copy-start(s32[9,9]{1,0:T(8,128)} %param.14) | copy-start | bytes 976
  41.4 7.5 %copy-start.4 = (s32[1,8]{1,0:T(1,128)S(1)}, s32[1,8]{1,0:T(1,128)}, u32[]{:S(2)}) copy-start(s32[1,8]{1,0:T(1,128)} %param.16) | copy-start | bytes 100
  41.5 1.6 %collective-permute-start = (bf16[128,1024]{1,0:T(8,128)(2,1)S(1)}, bf16[128,1024]{1,0:T(8,128)(2,1)S(1)}, u32[]{:S(2)}, u32[]{:S(2)}) collective-permute-start(bf16[128,1024]{1,0:T(8,128)(2,1)S(1)} %lend_corners.1), channel_id=1, source_target_pairs={{0,4},{8,12},{16,20},{24,28},{4,0},{12,8},{20,16},{28,24},{1,5},{9... | collective-permute-start | bytes 786440 | tf_op jit(solution)/shard_map/ppermute | solution.py:402
  44.9 23.4 %collective-permute-start.2 = (bf16[256,1024]{1,0:T(8,128)(2,1)}, bf16[256,1024]{1,0:T(8,128)(2,1)S(1)}, u32[]{:S(2)}, u32[]{:S(2)}) collective-permute-start(bf16[256,1024]{1,0:T(8,128)(2,1)} %get-tuple-element.16), channel_id=1, source_target_pairs={{8,0},{12,4},{0,8},{4,12},{24,16},{28,20},{16,24},{20,28},{9,1},{1... | collective-permute-start | bytes 1572872 | tf_op jit(solution)/shard_map/ppermute | solution.py:402
  46.4 24.0 %collective-permute-start.3 = (bf16[256,1024]{1,0:T(8,128)(2,1)}, bf16[256,1024]{1,0:T(8,128)(2,1)}, u32[]{:S(2)}, u32[]{:S(2)}) collective-permute-start(bf16[256,1024]{1,0:T(8,128)(2,1)} %get-tuple-element.17), channel_id=1, source_target_pairs={{16,8},{20,12},{8,16},{12,20},{17,9},{21,13},{9,17},{13,21},{18,10... | collective-permute-start | bytes 1572872 | tf_op jit(solution)/shard_map/ppermute | solution.py:402
  48.8 19.5 %collective-permute-start.1 = (bf16[192,1024]{1,0:T(8,128)(2,1)}, bf16[192,1024]{1,0:T(8,128)(2,1)S(1)}, u32[]{:S(2)}, u32[]{:S(2)}) collective-permute-start(bf16[192,1024]{1,0:T(8,128)(2,1)} %get-tuple-element.15), channel_id=1, source_target_pairs={{0,4},{8,12},{16,20},{24,28},{4,0},{12,8},{20,16},{28,24},{1,5},{9... | collective-permute-start | bytes 1179656 | tf_op jit(solution)/shard_map/ppermute | solution.py:402
  85.7 0.8 copy-start.2
  86.5 9.5 %copy-start.3 = (bf16[192,1024]{1,0:T(8,128)(2,1)S(1)}, bf16[192,1024]{1,0:T(8,128)(2,1)}, u32[]{:S(2)}) copy-start(bf16[192,1024]{1,0:T(8,128)(2,1)} %copy-done.2) | copy-start | bytes 1179652
  86.5 13.3 %collective-permute-start.5 = (bf16[256,1024]{1,0:T(8,128)(2,1)}, bf16[256,1024]{1,0:T(8,128)(2,1)S(1)}, u32[]{:S(2)}, u32[]{:S(2)}) collective-permute-start(bf16[256,1024]{1,0:T(8,128)(2,1)} %get-tuple-element.21), channel_id=1, source_target_pairs={{0,8},{4,12},{8,0},{12,4},{16,24},{20,28},{24,16},{28,20},{1,9},{5... | collective-permute-start | bytes 1572872 | tf_op jit(solution)/shard_map/ppermute | solution.py:405
  86.5 25.3 %collective-permute-start.6 = (bf16[256,1024]{1,0:T(8,128)(2,1)}, bf16[256,1024]{1,0:T(8,128)(2,1)S(1)}, u32[]{:S(2)}, u32[]{:S(2)}) collective-permute-start(bf16[256,1024]{1,0:T(8,128)(2,1)} %get-tuple-element.22), channel_id=1, source_target_pairs={{8,16},{12,20},{16,8},{20,12},{9,17},{13,21},{17,9},{21,13},{10,18... | collective-permute-start | bytes 1572872 | tf_op jit(solution)/shard_map/ppermute | solution.py:405
  91.0 23.6 %all-to-all-start.2 = ((bf16[4,144,512]{2,1,0:T(8,128)(2,1)}), bf16[4,144,512]{2,1,0:T(8,128)(2,1)S(1)}, u32[]{:S(2)}, u32[]{:S(2)}) async-start(bf16[4,144,512]{2,1,0:T(8,128)(2,1)} %bitcast.6), calls=%async_computation.2 | async-start | bytes 1179648 | tf_op jit(solution)/shard_map/all_to_all | solution.py:389
  96.0 17.4 %copy-start = (f32[2,576,512]{2,1,0:T(8,128)S(1)}, f32[2,576,512]{2,1,0:T(8,128)}, u32[]{:S(2)}) copy-start(f32[2,576,512]{2,1,0:T(8,128)} %get-tuple-element.19.refs_2_) | copy-start | bytes 7077892
  96.0 15.8 %collective-permute-start.4 = (bf16[192,1024]{1,0:T(8,128)(2,1)S(1)}, bf16[192,1024]{1,0:T(8,128)(2,1)S(1)}, u32[]{:S(2)}, u32[]{:S(2)}) collective-permute-start(bf16[192,1024]{1,0:T(8,128)(2,1)S(1)} %copy-done.3), channel_id=1, source_target_pairs={{4,0},{12,8},{20,16},{28,24},{0,4},{8,12},{16,20},{24,28},{5,1},{1... | collective-permute-start | bytes 1179656 | tf_op jit(solution)/shard_map/ppermute | solution.py:405
  111.8 1.6 %collective-permute-start.7 = (bf16[128,1024]{1,0:T(8,128)(2,1)S(1)}, bf16[128,1024]{1,0:T(8,128)(2,1)S(1)}, u32[]{:S(2)}, u32[]{:S(2)}) collective-permute-start(bf16[128,1024]{1,0:T(8,128)(2,1)S(1)} %forward.1), channel_id=1, source_target_pairs={{4,0},{12,8},{20,16},{28,24},{0,4},{8,12},{16,20},{24,28},{5,1},{1... | collective-permute-start | bytes 786440 | tf_op jit(solution)/shard_map/ppermute | solution.py:405
